TPU v7x, 128 devices: a whole 4x4x4 slice. The times are simulated.
128 devices in a mesh: fine: 32 (over z, x, core), sub: 4 (over y).
Axes of the slice: x: 4, y: 4, z: 4, core: 2. Of those that a mesh axis runs over, the one named last changes fastest.
Arguments:
- a_tiles: bfloat16 [4096, 8, 128, 128], P(('fine', 'sub')), may hold values from -5 to 5
- a_cols: int32 [4096, 8], P(('fine', 'sub')), may hold values from 0 to 4095, as said below
- a_count: int32 [4096], P(('fine', 'sub')), may hold values from 2 to 8
- p_tiles: bfloat16 [4096, 4, 128, 128], P(('fine', 'sub')), may hold values from -0.25 to 0.25
- p_cols: int32 [4096, 4], P(('fine', 'sub')), may hold values from 0 to 255, as said below
Outputs:
- coarse_op: float32 [256, 7, 128, 128], P('fine', None, 'sub')
Inputs may be any that keep to these rules, and one draw needn't show every extreme that they name: `a_cols`: each entry is within 16 of its row's index; slot 0 of every row is the row itself. `p_cols`: each entry is within one of its row's index divided by 16, rounded down.
All inputs are finite; a program needn't handle non-finite values.
Results may differ from a plain program's by a relative error of at most 0.0065.
Values may be sent and summed in bfloat16 or wider, within the bound.
No kernel may reach another device: no remote copies, remote signals or barrier semaphores. Data moves between devices by JAX's collectives and lax.ppermute only.
A program may use at most 128 MiB of HBM per device.

v0:
```python
import math

import jax
import jax.numpy as jnp
from jax import lax
from jax.sharding import PartitionSpec as P

A_SLOTS = 8
AGG_RATIO = 16
REACH = 16


def extended(block, sides, width):
    for axis, dim in sides:
        count = lax.axis_size(axis)
        forward = [(i, i + 1) for i in range(count - 1)]
        backward = [(target, source) for source, target in forward]
        low = lax.ppermute(
            lax.slice_in_dim(block, block.shape[dim] - width, None, axis=dim), axis, forward
        )
        high = lax.ppermute(lax.slice_in_dim(block, 0, width, axis=dim), axis, backward)
        block = jnp.concatenate([low, block, high], axis=dim)
    return block


def shifted(block, axis, distance):
    devices = range(lax.axis_size(axis))
    route = [(i - distance, i) for i in devices if i - distance in devices]
    return lax.ppermute(block, axis, route)


def shards(a_tiles, a_cols, a_count, p_tiles, p_cols):
    row_count = a_tiles.shape[0]
    tile_size = a_tiles.shape[2]
    slot_total = p_tiles.shape[1]
    sub_count = lax.axis_size("sub")
    coarse_dev = row_count * sub_count // AGG_RATIO
    window_rows = coarse_dev + 2
    device = lax.axis_index(("fine", "sub"))
    ext_tiles, ext_cols = (
        extended(p_tiles, ((("fine", "sub"), 0),), REACH),
        extended(p_cols, ((("fine", "sub"), 0),), REACH),
    )
    ext_wide = ext_tiles.transpose(0, 2, 1, 3).reshape(
        ext_tiles.shape[0], tile_size, slot_total * tile_size
    )
    first_row = device * row_count - REACH
    coarse_base = lax.axis_index("fine") * coarse_dev - 1
    block_rows = math.gcd(math.gcd(row_count, 2), AGG_RATIO)
    block_count = row_count // block_rows
    global_rows = device * row_count + jnp.arange(row_count, dtype=jnp.int32)
    slot_index = jnp.arange(A_SLOTS, dtype=jnp.int32)
    offset_index = jnp.arange(5, dtype=jnp.int32)
    shift_index = jnp.arange(-1, 2, dtype=jnp.int32)
    highest = lax.Precision.HIGHEST

    def blocked(value):
        return value.reshape((block_count, block_rows) + value.shape[1:])

    def step(total, items):
        a_block, col_block, used, own_tiles, own_cols, row_ids = items
        local_rows = col_block - first_row
        fetched = ext_wide[local_rows]
        fetched_cols = ext_cols[local_rows]
        agg_rows = row_ids // AGG_RATIO
        valid = slot_index[None, :] < used[:, None]
        rel_cols = fetched_cols - agg_rows[:, None, None] + 2
        picker = ((rel_cols[..., None] == offset_index) & valid[:, :, None, None]).astype(
            jnp.float32
        )
        products = jnp.einsum(
            "gkab,gkbn->gkan", a_block, fetched, preferred_element_type=jnp.float32
        )
        products = products.reshape(
            products.shape[0], products.shape[1], tile_size, slot_total, tile_size
        )
        ap_rows = jnp.einsum("gkmo,gkamc->goac", picker, products, precision=highest).astype(
            jnp.bfloat16
        )
        shift_rel = own_cols - agg_rows[:, None]
        select = (shift_rel[..., None] == shift_index).astype(jnp.bfloat16)
        own_masked = own_tiles[:, :, None] * select[:, :, :, None, None]
        summed_rows = jnp.einsum(
            "gmsba,gobc->soac", own_masked, ap_rows, preferred_element_type=jnp.float32
        )
        placed = []
        for shift in (-1, 0, 1):
            placed.append(jnp.pad(summed_rows[shift + 1], ((1 - shift, 1 + shift), (0, 0), (0, 0))))
        contrib = jnp.stack(placed)
        start = agg_rows[0] - 1 - coarse_base
        current = lax.dynamic_slice_in_dim(total, start, 3, 0)
        total = lax.dynamic_update_slice_in_dim(total, current + contrib, start, 0)
        return (total, None)

    initial = jnp.zeros((window_rows, 7, tile_size, tile_size), jnp.float32)
    items = (
        blocked(a_tiles),
        blocked(a_cols),
        blocked(a_count),
        blocked(p_tiles),
        blocked(p_cols),
        blocked(global_rows),
    )
    partial_value, unused = lax.scan(step, initial, items)
    summed = lax.psum_scatter(partial_value, "sub", scatter_dimension=2, tiled=True)
    from_below = shifted(summed[window_rows - 1 :], "fine", 1)
    from_above = shifted(summed[0:1], "fine", -1)
    owned = summed[1 : window_rows - 1]
    owned = owned.at[0].add(from_below[0])
    owned = owned.at[coarse_dev - 1].add(from_above[0])
    return owned


def solution(mesh):
    in_specs = (
        P(("fine", "sub"), None, None, None),
        P(("fine", "sub"), None),
        P(("fine", "sub")),
        P(("fine", "sub"), None, None, None),
        P(("fine", "sub"), None),
    )
    out_specs = P("fine", None, "sub", None)
    return jax.shard_map(shards, mesh=mesh, in_specs=in_specs, out_specs=out_specs, check_vma=False)
```

profile of v0, /device:TPU:38, one launch (start us, length us, event | category | flops | bytes accessed | tf_op | source)
XLA Modules:
  0.0 586.2 jit_solution(15799917251309968154)
XLA Ops:
  20.3 5.8 collective-permute-start.1
  26.3 33.0 %collective-permute-done = s32[16,4]{0,1:T(4,128)S(1)} collective-permute-done((s32[16,4]{0,1:T(4,128)S(1)}, s32[16,4]{0,1:T(4,128)S(1)}, u32[]{:S(2)}, u32[]{:S(2)}) %collective-permute-start) | collective-permute-done | bytes 288 | tf_op jit(solution)/shard_map/ppermute | solution.py:18
  63.4 7.1 %copy_bitcast_fusion = bf16[64,128,512]{2,1,0:T(8,128)(2,1)} fusion(bf16[16,4,128,128]{3,2,1,0:T(8,128)(2,1)} %collective-permute-done.3, bf16[32,4,128,128]{3,2,1,0:T(8,128)(2,1)} %param.14, bf16[16,4,128,128]{3,2,1,0:T(8,128)(2,1)} %collective-permute-done.2), kind=kLoop, calls=%fused_computation.52 | loop fusion | flops 8388608 | bytes 16777216 | tf_op jit(solution)/shard_map/reshape | solution.py:44
  73.2 443.1 %while.16 = (s32[]{:T(128)}, f32[10,7,128,128]{3,2,1,0:T(8,128)}, s32[16,2]{1,0:T(8,128)S(1)}, s32[]{:T(128)}, s32[16,2,8]{2,1,0:T(2,128)S(1)}, /*index=5*/s32[]...) while((s32[]{:T(128)}, f32[10,7,128,128]{3,2,1,0:T(8,128)}, ...), condition=%wide.region_2.3_spmd.clone, body=%wide.region_0.2_spmd.clone.sunk | while | flops 460244928 | bytes 45883100 | solution.py:104
  87.2 5.3 fusion.52
  115.0 5.3 fusion.52
  137.4 5.3 reshape.314
  142.7 5.3 fusion.52
  170.5 5.3 fusion.52
  198.2 5.3 fusion.52
  220.6 5.3 reshape.314
  225.9 5.3 fusion.52
  253.7 5.3 fusion.52
  281.4 5.3 fusion.52
  303.8 5.3 reshape.314
  309.2 5.3 fusion.52
  336.8 5.3 fusion.52
  364.5 5.3 fusion.52
  392.1 5.3 fusion.52
  419.8 5.3 fusion.52
  447.4 5.3 fusion.52
  475.1 5.3 fusion.52
  502.7 5.3 fusion.52
  516.4 52.4 %reduce-scatter.2.cloned.1.call-done = f32[10,7,32,128]{3,2,1,0:T(8,128)} async-done(((f32[10,7,128,128]{3,2,1,0:T(8,128)}), f32[10,7,32,128]{3,2,1,0:T(8,128)}) %reduce-scatter.2.cloned.1.call-update) | async-done | bytes 1146896 | tf_op jit(solution)/shard_map/reduce_scatter | solution.py:105
  (465 shorter events, 371.5 us)
Async XLA Ops:
  6.5 11.7 %copy-start.2 = (s32[32,4]{0,1:T(4,128)S(1)}, s32[32,4]{0,1:T(4,128)}, u32[]{:S(2)}) copy-start(s32[32,4]{0,1:T(4,128)} %param.15) | copy-start | bytes 1540
  6.5 19.6 %copy-start.3 = (s32[32,8]{0,1:T(8,128)S(1)}, s32[32,8]{0,1:T(8,128)}, u32[]{:S(2)}) copy-start(s32[32,8]{0,1:T(8,128)} %param.12) | copy-start | bytes 3076
  6.5 19.7 %copy-start.4 = (s32[32]{0:T(128)S(1)}, s32[32]{0:T(128)}, u32[]{:S(2)}) copy-start(s32[32]{0:T(128)} %param.13) | copy-start | bytes 388
  6.5 562.2 %reduce-scatter.2.cloned.1.call-start = ((), (), s32[]{:S(2)}) async-start(), calls=%async_computation.1 | async-start | bytes 5734400 | tf_op jit(solution)/shard_map/reduce_scatter | solution.py:105
  10.6 52.8 %collective-permute-start.2 = (bf16[16,4,128,128]{3,2,1,0:T(8,128)(2,1)}, bf16[16,4,128,128]{3,2,1,0:T(8,128)(2,1)}, u32[]{:S(2)}, u32[]{:S(2)}) collective-permute-start(bf16[16,4,128,128]{3,2,1,0:T(8,128)(2,1)} %get-tuple-element.338), channel_id=1, source_target_pairs={{0,1},{1,2},{2,3},{3,4},{4,5},{5,6},{6,7},{7,8},{8,9},{9,10},{10,1... | collective-permute-start | bytes 6291464 | tf_op jit(solution)/shard_map/ppermute | solution.py:18
  14.1 49.3 %collective-permute-start.3 = (bf16[16,4,128,128]{3,2,1,0:T(8,128)(2,1)S(1)}, bf16[16,4,128,128]{3,2,1,0:T(8,128)(2,1)}, u32[]{:S(2)}, u32[]{:S(2)}) collective-permute-start(bf16[16,4,128,128]{3,2,1,0:T(8,128)(2,1)S(1)} %get-tuple-element.339), channel_id=1, source_target_pairs={{1,0},{2,1},{3,2},{4,3},{5,4},{6,5},{7,6},{8,7},{9,8},{10,9},{11,1... | collective-permute-start | bytes 6291464 | tf_op jit(solution)/shard_map/ppermute | solution.py:21
  18.3 40.9 %collective-permute-start = (s32[16,4]{0,1:T(4,128)S(1)}, s32[16,4]{0,1:T(4,128)S(1)}, u32[]{:S(2)}, u32[]{:S(2)}) collective-permute-start(s32[16,4]{0,1:T(4,128)S(1)} %get-tuple-element.342), channel_id=1, source_target_pairs={{0,1},{1,2},{2,3},{3,4},{4,5},{5,6},{6,7},{7,8},{8,9},{9,10},{10,1... | collective-permute-start | bytes 776 | tf_op jit(solution)/shard_map/ppermute | solution.py:18
  20.3 42.9 %collective-permute-start.1 = (s32[16,4]{0,1:T(4,128)S(1)}, s32[16,4]{0,1:T(4,128)S(1)}, u32[]{:S(2)}, u32[]{:S(2)}) collective-permute-start(s32[16,4]{0,1:T(4,128)S(1)} %get-tuple-element.343), channel_id=1, source_target_pairs={{1,0},{2,1},{3,2},{4,3},{5,4},{6,5},{7,6},{8,7},{9,8},{10,9},{11,1... | collective-permute-start | bytes 776 | tf_op jit(solution)/shard_map/ppermute | solution.py:21
  568.8 7.2 %copy-start = (f32[10,7,32,128]{3,2,1,0:T(8,128)S(1)}, f32[10,7,32,128]{3,2,1,0:T(8,128)}, u32[]{:S(2)}) copy-start(f32[10,7,32,128]{3,2,1,0:T(8,128)} %reduce-scatter.2.cloned.1.call-done) | copy-start | bytes 3440644
  568.8 7.2 %slice-start = ((f32[10,7,32,128]{3,2,1,0:T(8,128)}), f32[8,7,32,128]{3,2,1,0:T(8,128)S(1)}, s32[]{:S(2)}) async-start(f32[10,7,32,128]{3,2,1,0:T(8,128)} %reduce-scatter.2.cloned.1.call-done), calls=%async_computation.2 | async-start | bytes 1835008 | tf_op jit(solution)/shard_map/slice | solution.py:108
  569.9 6.1 %collective-permute-start.4 = (f32[1,7,32,128]{3,2,1,0:T(8,128)S(1)}, f32[1,7,32,128]{3,2,1,0:T(8,128)S(1)}, u32[]{:S(2)}, u32[]{:S(2)}) collective-permute-start(f32[1,7,32,128]{3,2,1,0:T(8,128)S(1)} %get-tuple-element.341), channel_id=1, source_target_pairs={{0,4},{4,8},{8,12},{12,16},{16,20},{20,24},{24,28},{28,32},{32,36}... | collective-permute-start | bytes 344072 | tf_op jit(solution)/shard_map/ppermute | solution.py:29
  571.8 6.0 %collective-permute-start.5 = (f32[1,7,32,128]{3,2,1,0:T(8,128)S(1)}, f32[1,7,32,128]{3,2,1,0:T(8,128)S(1)}, u32[]{:S(2)}, u32[]{:S(2)}) collective-permute-start(f32[1,7,32,128]{3,2,1,0:T(8,128)S(1)} %get-tuple-element.340), channel_id=1, source_target_pairs={{4,0},{8,4},{12,8},{16,12},{20,16},{24,20},{28,24},{32,28},{36,32}... | collective-permute-start | bytes 344072 | tf_op jit(solution)/shard_map/ppermute | solution.py:29
  576.0 1.8 copy-start.1
Sparse Core Ops, SparseCore 0:
  516.5 52.2 reduce-scatter.1
where the time goes:
time: 596 us; the launch traced here: 586 us
  local copies, waits for them, and re-layouts  270 us (45%)
  matrix products  150 us (25%)
  waiting for transfers between devices  91.6 us (15%)
  other arithmetic  37.9 us (6%)
  starting transfers between devices  20.9 us (4%)
  between operations  13.5 us (2%)
    dot_general x16, matrix products, step(): jnp.einsum('gkmo,gkamc->goac', picker, products, precision=highest)  85.6 us
    reshape x16, local copies, waits for them, and re-layouts, step(): products.reshape(products.shape[0], products.shape[1], tile_size, slot_to...  84.2 us
    gather x16, local copies, waits for them, and re-layouts, step(): fetched = ext_wide[local_rows]  65 us
    dot_general x16, matrix products, step(): jnp.einsum('gkab,gkbn->gkan', a_block, fetched, preferred_element_type=jn...  58.9 us
    reduce_scatter x1, waiting for transfers between devices, shards(): lax.psum_scatter(partial_value, 'sub', scatter_dimension=2, tiled=True)  52.4 us
    ppermute x2, waiting for transfers between devices, extended(): lax.ppermute(lax.slice_in_dim(block, block.shape[dim] - width, None, axis...  33 us
    dynamic_slice x32, local copies, waits for them, and re-layouts, step(): current = lax.dynamic_slice_in_dim(total, start, 3, 0)  29.9 us
    another operation x32, local copies, waits for them, and re-layouts, step(): contrib = jnp.stack(placed)  26.6 us
  transfers between devices with their start and end apart: 7, of which 5 were waited for; matrix products, arithmetic and copies ran while one was open for 0% of the time, Pallas kernels for 0%

commit v1 on v0

v1 whole, which is shorter than its diff:
```python
import jax
import jax.numpy as jnp
from jax import lax
from jax.experimental import pallas as pl
from jax.experimental.pallas import tpu as pltpu
from jax.sharding import PartitionSpec as P

AGG = 16
TILE = 128
SLOTS_A = 8
SLOTS_P = 4
ROWS = 32
SUBS = 4
F32 = jnp.float32
BF16 = jnp.bfloat16
MIB = 1 << 20


def place():
    fine = lax.axis_index("fine")
    sub = lax.axis_index("sub")
    return fine * SUBS + sub, sub, lax.rem(sub, 2)


def collapse_kernel(cols, p_ref, pc_ref, *sent):
    step = pl.program_id(0)
    steps = pl.num_programs(0)
    rows = p_ref.shape[0]
    device, sub, parity = place()
    half = step // (steps // 2)
    agg = device * 2 + half
    by_b = half ^ (1 - parity)
    for r in range(rows):
        row = step * rows + r
        local = row - half * AGG
        tiles = [p_ref[r, k].astype(F32) for k in range(SLOTS_P)]
        rel = [cols[row, k] - agg for k in range(SLOTS_P)]
        for c in range(3):
            m = jnp.where(half == 1, 1 - c, c - 1)
            value = jnp.where(rel[0] == m, tiles[0], 0.0)
            for k in range(1, SLOTS_P):
                value = value + jnp.where(rel[k] == m, tiles[k], 0.0)
            value = value.astype(BF16)
            pc_ref[m + 1, r] = value

            @pl.when(by_b == 0)
            def _():
                sent[c][local] = value

            @pl.when(by_b == 1)
            def _():
                sent[3 + c][local] = value


def collapse(p_tiles, p_cols):
    rows = 4
    message = jax.ShapeDtypeStruct((AGG, TILE, TILE), BF16)
    whole = pl.BlockSpec((AGG, TILE, TILE), lambda i, *_: (0, 0, 0))
    return pl.pallas_call(
        collapse_kernel,
        out_shape=[jax.ShapeDtypeStruct((3, ROWS, TILE, TILE), BF16)] + [message] * 6,
        grid_spec=pltpu.PrefetchScalarGridSpec(
            num_scalar_prefetch=1,
            grid=(ROWS // rows,),
            in_specs=[pl.BlockSpec((rows, SLOTS_P, TILE, TILE), lambda i, *_: (i, 0, 0, 0))],
            out_specs=[pl.BlockSpec((3, rows, TILE, TILE), lambda i, *_: (0, i, 0, 0))]
            + [whole] * 6,
        ),
        compiler_params=pltpu.CompilerParams(vmem_limit_bytes=24 * MIB),
        cost_estimate=pl.CostEstimate(flops=12 * MIB, bytes_accessed=10 * MIB, transcendentals=0),
    )(p_cols, p_tiles)


def local_kernel(acols, acount, a_ref, pc_ref, out_ref, rh_ref, total):
    step = pl.program_id(0)
    steps = pl.num_programs(0)
    rows = a_ref.shape[0]
    device, sub, parity = place()
    half = step // (steps // 2)
    inner = lax.rem(step, steps // 2)
    base = device * ROWS + half * AGG - AGG

    @pl.when(inner == 0)
    def _():
        def clear(i, carry):
            total[i] = jnp.zeros((3 * TILE, TILE), F32)
            return carry

        lax.fori_loop(0, 3 * AGG, clear, 0)

    for r in range(rows):
        row = step * rows + r
        own = jnp.concatenate([pc_ref[m, row].T for m in range(3)], axis=0)
        used = acount[row]
        for k in range(0, SLOTS_A, 2):
            pair = jnp.concatenate([a_ref[r, k], a_ref[r, k + 1]], axis=1)
            both = jnp.dot(own, pair, preferred_element_type=F32)
            for e in range(2):
                at = jnp.where(k + e < used, acols[row, k + e] - base, 3 * AGG)
                total[at] += both[:, e * TILE : (e + 1) * TILE]

    @pl.when(inner == steps // 2 - 1)
    def _():
        for c in range(AGG):
            rh_ref[0, :, c * TILE : (c + 1) * TILE] = total[32 * half + c].astype(BF16)
        out_ref[...] = jnp.zeros_like(out_ref)
        for b in range(2):
            first = AGG * (b - half + 1)
            left = jnp.concatenate([total[first + c].astype(BF16) for c in range(AGG)], axis=1)
            right = jnp.concatenate(
                [pc_ref[m, AGG * b : AGG * (b + 1)].reshape(AGG * TILE, TILE) for m in range(3)],
                axis=1,
            )
            part = jnp.dot(left, right, preferred_element_type=F32)
            for m in range(3):
                out_ref[0, b - half + 1 + m] += part[:, m * TILE : (m + 1) * TILE]


def local_part(a_tiles, a_cols, a_count, pc):
    rows = 4
    half_steps = ROWS // rows // 2
    return pl.pallas_call(
        local_kernel,
        out_shape=[
            jax.ShapeDtypeStruct((2, 5, 3 * TILE, TILE), F32),
            jax.ShapeDtypeStruct((2, 3 * TILE, AGG * TILE), BF16),
        ],
        grid_spec=pltpu.PrefetchScalarGridSpec(
            num_scalar_prefetch=2,
            grid=(ROWS // rows,),
            in_specs=[
                pl.BlockSpec((rows, SLOTS_A, TILE, TILE), lambda i, *_: (i, 0, 0, 0)),
                pl.BlockSpec((3, ROWS, TILE, TILE), lambda i, *_: (0, 0, 0, 0)),
            ],
            out_specs=[
                pl.BlockSpec((1, 5, 3 * TILE, TILE), lambda i, *_: (i // half_steps, 0, 0, 0)),
                pl.BlockSpec((1, 3 * TILE, AGG * TILE), lambda i, *_: (i // half_steps, 0, 0)),
            ],
            scratch_shapes=[pltpu.VMEM((3 * AGG + 1, 3 * TILE, TILE), F32)],
        ),
        compiler_params=pltpu.CompilerParams(vmem_limit_bytes=44 * MIB),
        cost_estimate=pl.CostEstimate(
            flops=8 * 1024 * MIB, bytes_accessed=16 * MIB, transcendentals=0
        ),
    )(a_cols, a_count, a_tiles, pc)


def finish_kernel(chunk, ha_ref, hb_ref, rh_ref, out_ref, mine, to1, to2, to3, tiles):
    device, sub, parity = place()
    count = tiles.shape[1]
    for x, halo in enumerate((ha_ref, hb_ref)):
        side = x ^ (1 - parity)
        part = jnp.dot(
            rh_ref[side], halo[...].reshape(AGG * TILE, TILE), preferred_element_type=F32
        )
        part = part + out_ref[side, jnp.where(side == 0, 2 - chunk, 2 + chunk)]
        if chunk < 2:
            other = out_ref[1 - side, jnp.where(side == 0, 1 - chunk, 3 + chunk)]
            low = jnp.where(side == 0, part, other)
            high = jnp.where(side == 0, other, part)
            tiles[side, 0] = low[:TILE]
            tiles[side, 1] = low[TILE : 2 * TILE] + high[:TILE]
            tiles[side, 2] = low[2 * TILE :] + high[TILE : 2 * TILE]
            tiles[side, 3] = high[2 * TILE :]
        else:
            for t in range(3):
                tiles[side, t] = part[t * TILE : (t + 1) * TILE]
    wide = TILE // SUBS
    for d, target in enumerate((mine, to1, to2, to3)):
        rows = pl.ds(pl.multiple_of((sub ^ d) * wide, wide), wide)
        for side in range(2):
            for i in range(count):
                target[side, i] = tiles[side, i, rows, :].astype(target.dtype)


def finish_chunk(chunk, ha, hb, rh, local):
    count = 4 if chunk < 2 else 3
    shape = (2, count, TILE // SUBS, TILE)

    def kernel(*refs):
        finish_kernel(chunk, *refs)

    return pl.pallas_call(
        kernel,
        out_shape=[jax.ShapeDtypeStruct(shape, F32)] + [jax.ShapeDtypeStruct(shape, BF16)] * 3,
        in_specs=[pl.BlockSpec(memory_space=pltpu.VMEM)] * 4,
        out_specs=[pl.BlockSpec(memory_space=pltpu.VMEM)] * 4,
        scratch_shapes=[pltpu.VMEM((2, count, TILE, TILE), F32)],
        compiler_params=pltpu.CompilerParams(vmem_limit_bytes=24 * MIB),
        cost_estimate=pl.CostEstimate(
            flops=400 * MIB, bytes_accessed=6 * MIB, transcendentals=0
        ),
    )(ha, hb, rh, local)


def gather_kernel(*refs):
    parts, (out_ref, below_ref, above_ref, window) = refs[:12], refs[12:]
    device, sub, parity = place()
    window[...] = jnp.zeros_like(window)
    for chunk in range(3):
        for d in range(4):
            part = parts[chunk * 4 + d]
            first = 2 * (sub ^ d)
            for side in range(2):
                column = 1 + chunk if side else -chunk
                for t in range(part.shape[1]):
                    i = t if chunk < 2 else t + side
                    if 0 <= column - i + 4 < 7:
                        window[first + i, column - i + 4] += part[side, t].astype(F32)
    out_ref[...] = window[1:9]
    below_ref[...] = window[0].astype(BF16)
    above_ref[...] = window[9].astype(BF16)


def gather_parts(parts):
    wide = TILE // SUBS
    edge = jax.ShapeDtypeStruct((7, wide, TILE), BF16)
    return pl.pallas_call(
        gather_kernel,
        out_shape=[jax.ShapeDtypeStruct((8, 7, wide, TILE), F32), edge, edge],
        in_specs=[pl.BlockSpec(memory_space=pltpu.VMEM)] * 12,
        out_specs=[pl.BlockSpec(memory_space=pltpu.VMEM)] * 3,
        scratch_shapes=[pltpu.VMEM((10, 7, wide, TILE), F32)],
        compiler_params=pltpu.CompilerParams(vmem_limit_bytes=16 * MIB),
    )(*parts)


def edge_kernel(from_below, from_above, whole_ref, out_ref):
    out_ref[...] = whole_ref[...]
    out_ref[0] += from_below[...].astype(F32)
    out_ref[7] += from_above[...].astype(F32)


def add_edges(from_below, from_above, whole):
    return pl.pallas_call(
        edge_kernel,
        out_shape=jax.ShapeDtypeStruct(whole.shape, F32),
        in_specs=[pl.BlockSpec(memory_space=pltpu.VMEM)] * 3,
        out_specs=pl.BlockSpec(memory_space=pltpu.VMEM),
        compiler_params=pltpu.CompilerParams(vmem_limit_bytes=16 * MIB),
    )(from_below, from_above, whole)


def shards(a_tiles, a_cols, a_count, p_tiles, p_cols):
    fines = lax.axis_size("fine")
    total = fines * SUBS
    pc, *sent = collapse(p_tiles, p_cols)
    pairs_a = [(i, i ^ 1) for i in range(total)]
    pairs_b = [(i, i + 1) for i in range(1, total - 1, 2)]
    pairs_b = pairs_b + [(b, a) for a, b in pairs_b]
    both = ("fine", "sub")
    halo = []
    for c in range(3):
        halo.append(
            (lax.ppermute(sent[c], both, pairs_a), lax.ppermute(sent[3 + c], both, pairs_b))
        )
    local, rh = local_part(a_tiles, a_cols, a_count, pc)
    parts = []
    for c in range(3):
        mine, *out = finish_chunk(c, halo[c][0], halo[c][1], rh, local)
        parts.append(mine)
        for d in range(3):
            route = [(i, i ^ (d + 1)) for i in range(SUBS)]
            parts.append(lax.ppermute(out[d], "sub", route))
    whole, below, above = gather_parts(parts)
    from_above = lax.ppermute(below, "fine", [(i + 1, i) for i in range(fines - 1)])
    from_below = lax.ppermute(above, "fine", [(i, i + 1) for i in range(fines - 1)])
    return add_edges(from_below, from_above, whole)


def solution(mesh):
    in_specs = (
        P(("fine", "sub"), None, None, None),
        P(("fine", "sub"), None),
        P(("fine", "sub")),
        P(("fine", "sub"), None, None, None),
        P(("fine", "sub"), None),
    )
    out_specs = P("fine", None, "sub", None)
    return jax.shard_map(shards, mesh=mesh, in_specs=in_specs, out_specs=out_specs, check_vma=False)
```

time: 596 us -> 84.3 us (0.14)
  the two profiles are of different devices: /device:TPU:38 before, /device:TPU:39 now
where the time goes in v1:
time: 84.3 us; the launch traced here: 83.9 us
  starting transfers between devices  35.6 us (42%)
  Pallas kernels  28.3 us (34%)
  waiting for transfers between devices  12.5 us (15%)
  local copies, waits for them, and re-layouts  7.38 us (9%)
    pallas_call x1, Pallas kernels, local_part(): pl.pallas_call(local_kernel, out_shape=[jax.ShapeDtypeStruct((2, 5, 3 * T...  18.6 us
    ppermute x3, starting transfers between devices, shards(): lax.ppermute(sent[3 + c], both, pairs_b)  14.9 us
    ppermute x9, starting transfers between devices, shards(): parts.append(lax.ppermute(out[d], 'sub', route))  10.3 us
    unnamed x14, local copies, waits for them, and re-layouts  7.38 us
    ppermute x1, starting transfers between devices, shards(): lax.ppermute(above, 'fine', [(i, i + 1) for i in range(fines - 1)])  6.92 us
    ppermute x1, waiting for transfers between devices, shards(): lax.ppermute(below, 'fine', [(i + 1, i) for i in range(fines - 1)])  5.67 us
    pallas_call x1, Pallas kernels, collapse(): pl.pallas_call(collapse_kernel, out_shape=[jax.ShapeDtypeStruct((3, ROWS,...  5.35 us
    ppermute x3, waiting for transfers between devices, shards(): lax.ppermute(sent[c], both, pairs_a)  3.67 us
  transfers between devices with their start and end apart: 17, of which 5 were waited for; matrix products, arithmetic and copies ran while one was open for 0% of the time, Pallas kernels for 26%

profile of v1, /device:TPU:39, one launch (start us, length us, event | category | flops | bytes accessed | tf_op | source)
XLA Modules:
  0.0 83.9 jit_solution(13680572371884966775)
XLA Ops:
  0.8 2.2 %copy-done = bf16[32,4,128,128]{3,2,1,0:T(8,128)(2,1)S(1)} copy-done((bf16[32,4,128,128]{3,2,1,0:T(8,128)(2,1)S(1)}, bf16[32,4,128,128]{3,2,1,0:T(8,128)(2,1)}, u32[]{:S(2)}) %copy-start) | copy-done | bytes 4194328
  3.0 5.4 %shard_map.55 = (bf16[3,32,128,128]{3,2,1,0:T(8,128)(2,1)S(1)}, bf16[16,128,128]{2,1,0:T(8,128)(2,1)}, bf16[16,128,128]{2,1,0:T(8,128)(2,1)}, bf16[16,128,128]{2...) custom-call(s32[32,4]{1,0:T(8,128)S(1)} %copy.6.cols, ...), custom_call_target="tpu_custom_call" | custom-call | flops 12582912 | bytes 10485760 | tf_op jit(solution)/shard_map/pallas_call | solution.py:59
  8.3 1.6 %copy-done.1 = bf16[3,32,128,128]{3,2,1,0:T(8,128)(2,1)} copy-done((bf16[3,32,128,128]{3,2,1,0:T(8,128)(2,1)}, bf16[3,32,128,128]{3,2,1,0:T(8,128)(2,1)S(1)}, u32[]{:S(2)}) %copy-start.1) | copy-done | bytes 3145752
  10.8 1.3 %collective-permute-start.5 = (bf16[16,128,128]{2,1,0:T(8,128)(2,1)}, bf16[16,128,128]{2,1,0:T(8,128)(2,1)S(1)}, u32[]{:S(2)}, u32[]{:S(2)}) collective-permute-start(bf16[16,128,128]{2,1,0:T(8,128)(2,1)} %get-tuple-element.38), channel_id=1, source_target_pairs={{0,1},{1,0},{2,3},{3,2},{4,5},{5,4},{6,7},{7,6},{8,9},{9,8},{10,11... | collective-permute-start | bytes 1572872 | tf_op jit(solution)/shard_map/ppermute | solution.py:255
  12.2 5.8 %collective-permute-start.1 = (bf16[16,128,128]{2,1,0:T(8,128)(2,1)S(1)}, bf16[16,128,128]{2,1,0:T(8,128)(2,1)S(1)}, u32[]{:S(2)}, u32[]{:S(2)}) collective-permute-start(bf16[16,128,128]{2,1,0:T(8,128)(2,1)S(1)} %get-tuple-element.30), channel_id=1, source_target_pairs={{1,2},{3,4},{5,6},{7,8},{9,10},{11,12},{13,14},{15,16},{17,18},{19... | collective-permute-start | bytes 1572872 | tf_op jit(solution)/shard_map/ppermute | solution.py:255
  18.0 1.9 %collective-permute-start.6 = (bf16[16,128,128]{2,1,0:T(8,128)(2,1)}, bf16[16,128,128]{2,1,0:T(8,128)(2,1)S(1)}, u32[]{:S(2)}, u32[]{:S(2)}) collective-permute-start(bf16[16,128,128]{2,1,0:T(8,128)(2,1)} %get-tuple-element.39), channel_id=1, source_target_pairs={{1,2},{3,4},{5,6},{7,8},{9,10},{11,12},{13,14},{15,16},{17,18},{19... | collective-permute-start | bytes 1572872 | tf_op jit(solution)/shard_map/ppermute | solution.py:255
  20.1 3.7 %collective-permute-done.5.refs_0_ = bf16[16,128,128]{2,1,0:T(8,128)(2,1)S(1)} collective-permute-done((bf16[16,128,128]{2,1,0:T(8,128)(2,1)}, bf16[16,128,128]{2,1,0:T(8,128)(2,1)S(1)}, u32[]{:S(2)}, u32[]{:S(2)}) %collective-permute-start.5) | collective-permute-done | bytes 524320 | tf_op jit(solution)/shard_map/ppermute | solution.py:255
  23.8 7.2 %collective-permute-start.11 = (bf16[16,128,128]{2,1,0:T(8,128)(2,1)}, bf16[16,128,128]{2,1,0:T(8,128)(2,1)S(1)}, u32[]{:S(2)}, u32[]{:S(2)}) collective-permute-start(bf16[16,128,128]{2,1,0:T(8,128)(2,1)} %copy-done.3), channel_id=1, source_target_pairs={{1,2},{3,4},{5,6},{7,8},{9,10},{11,12},{13,14},{15,16},{17,18},{19... | collective-permute-start | bytes 1572872 | tf_op jit(solution)/shard_map/ppermute | solution.py:255
  31.0 1.9 %copy-done.2 = bf16[3,32,128,128]{3,2,1,0:T(8,128)(2,1)S(1)} copy-done((bf16[3,32,128,128]{3,2,1,0:T(8,128)(2,1)S(1)}, bf16[3,32,128,128]{3,2,1,0:T(8,128)(2,1)}, u32[]{:S(2)}) %copy-start.2) | copy-done | bytes 3145752
  32.9 18.6 %shard_map.56 = (f32[2,5,384,128]{3,2,1,0:T(8,128)S(1)}, bf16[2,384,2048]{2,1,0:T(8,128)(2,1)S(1)}) custom-call(s32[32,8]{1,0:T(8,128)S(1)} %copy.7.acols, s32[32]{0:T(128)S(1)} %copy-done.4, bf16[32,8,128,128]{3,2,1,0:T(8,128)(2,1)} %a_ref.1, bf16[3,32,128,128]{3,2,1,0:T(8,128)(2,1)S(1)} %copy-done.2), custom_call_target="tpu_custom_call" | custom-call | flops 8589934592 | bytes 16777216 | tf_op jit(solution)/shard_map/pallas_call | solution.py:122
  51.6 1.0 %shard_map.58 = (f32[2,4,32,128]{3,2,1,0:T(8,128)S(1)}, bf16[2,4,32,128]{3,2,1,0:T(8,128)(2,1)S(1)}, bf16[2,4,32,128]{3,2,1,0:T(8,128)(2,1)S(1)}, bf16[2,4,32,128]{3,2,1,0:T(8,128)(2,1)S(1)}) custom-call(bf16[16,128,128]{2,1,0:T(8,128)(2,1)S(1)} %collective-permute-done.5.refs_0_, bf16[16,128,128]{2,1,0:T(8,128)(2,1)S(1)} %collective-permute-done.6.refs_1_, ...), custom_call_target="tpu_custom_call" | custom-call | flops 419430400 | bytes 6291456 | tf_op jit(solution)/shard_map/pallas_call | solution.py:183
  52.9 1.0 %shard_map.59 = (f32[2,3,32,128]{3,2,1,0:T(8,128)S(1)}, bf16[2,3,32,128]{3,2,1,0:T(8,128)(2,1)S(1)}, bf16[2,3,32,128]{3,2,1,0:T(8,128)(2,1)S(1)}, bf16[2,3,32,128]{3,2,1,0:T(8,128)(2,1)S(1)}) custom-call(bf16[16,128,128]{2,1,0:T(8,128)(2,1)S(1)} %collective-permute-done.10.refs_0_, bf16[16,128,128]{2,1,0:T(8,128)(2,1)S(1)} %collective-permute-done.11.refs_1_, ...), custom_call_target="tpu_custom_call" | custom-call | flops 419430400 | bytes 6291456 | tf_op jit(solution)/shard_map/pallas_call | solution.py:183
  54.0 1.3 %collective-permute-start.12 = (bf16[2,3,32,128]{3,2,1,0:T(8,128)(2,1)S(1)}, bf16[2,3,32,128]{3,2,1,0:T(8,128)(2,1)S(1)}, u32[]{:S(2)}, u32[]{:S(2)}) collective-permute-start(bf16[2,3,32,128]{3,2,1,0:T(8,128)(2,1)S(1)} %get-tuple-element.47), channel_id=1, source_target_pairs={{0,1},{1,0},{2,3},{3,2},{4,5},{5,4},{6,7},{7,6},{8,9},{9,8},{10,11... | collective-permute-start | bytes 147464 | tf_op jit(solution)/shard_map/ppermute | solution.py:264
  55.2 1.0 %collective-permute-start.13 = (bf16[2,3,32,128]{3,2,1,0:T(8,128)(2,1)S(1)}, bf16[2,3,32,128]{3,2,1,0:T(8,128)(2,1)S(1)}, u32[]{:S(2)}, u32[]{:S(2)}) collective-permute-start(bf16[2,3,32,128]{3,2,1,0:T(8,128)(2,1)S(1)} %get-tuple-element.48), channel_id=1, source_target_pairs={{0,2},{1,3},{2,0},{3,1},{4,6},{5,7},{6,4},{7,5},{8,10},{9,11},{10,... | collective-permute-start | bytes 147464 | tf_op jit(solution)/shard_map/ppermute | solution.py:264
  56.3 1.6 %collective-permute-start.14 = (bf16[2,3,32,128]{3,2,1,0:T(8,128)(2,1)S(1)}, bf16[2,3,32,128]{3,2,1,0:T(8,128)(2,1)S(1)}, u32[]{:S(2)}, u32[]{:S(2)}) collective-permute-start(bf16[2,3,32,128]{3,2,1,0:T(8,128)(2,1)S(1)} %get-tuple-element.49), channel_id=1, source_target_pairs={{0,3},{1,2},{2,1},{3,0},{4,7},{5,6},{6,5},{7,4},{8,11},{9,10},{10,... | collective-permute-start | bytes 147464 | tf_op jit(solution)/shard_map/ppermute | solution.py:264
  58.8 1.0 %shard_map.57 = (f32[2,4,32,128]{3,2,1,0:T(8,128)S(1)}, bf16[2,4,32,128]{3,2,1,0:T(8,128)(2,1)S(1)}, bf16[2,4,32,128]{3,2,1,0:T(8,128)(2,1)S(1)}, bf16[2,4,32,128]{3,2,1,0:T(8,128)(2,1)S(1)}) custom-call(bf16[16,128,128]{2,1,0:T(8,128)(2,1)S(1)} %collective-permute-done.refs_0_, bf16[16,128,128]{2,1,0:T(8,128)(2,1)S(1)} %collective-permute-done.1.refs_1_, ...), custom_call_target="tpu_custom_call" | custom-call | flops 419430400 | bytes 6291456 | tf_op jit(solution)/shard_map/pallas_call | solution.py:183
  59.9 1.5 %collective-permute-start.9 = (bf16[2,4,32,128]{3,2,1,0:T(8,128)(2,1)S(1)}, bf16[2,4,32,128]{3,2,1,0:T(8,128)(2,1)S(1)}, u32[]{:S(2)}, u32[]{:S(2)}) collective-permute-start(bf16[2,4,32,128]{3,2,1,0:T(8,128)(2,1)S(1)} %get-tuple-element.43), channel_id=1, source_target_pairs={{0,3},{1,2},{2,1},{3,0},{4,7},{5,6},{6,5},{7,4},{8,11},{9,10},{10,... | collective-permute-start | bytes 196616 | tf_op jit(solution)/shard_map/ppermute | solution.py:264
  61.7 2.1 %collective-permute-start.3 = (bf16[2,4,32,128]{3,2,1,0:T(8,128)(2,1)S(1)}, bf16[2,4,32,128]{3,2,1,0:T(8,128)(2,1)S(1)}, u32[]{:S(2)}, u32[]{:S(2)}) collective-permute-start(bf16[2,4,32,128]{3,2,1,0:T(8,128)(2,1)S(1)} %get-tuple-element.36), channel_id=1, source_target_pairs={{0,2},{1,3},{2,0},{3,1},{4,6},{5,7},{6,4},{7,5},{8,10},{9,11},{10,... | collective-permute-start | bytes 196616 | tf_op jit(solution)/shard_map/ppermute | solution.py:264
  63.8 1.5 %collective-permute-start.4 = (bf16[2,4,32,128]{3,2,1,0:T(8,128)(2,1)S(1)}, bf16[2,4,32,128]{3,2,1,0:T(8,128)(2,1)S(1)}, u32[]{:S(2)}, u32[]{:S(2)}) collective-permute-start(bf16[2,4,32,128]{3,2,1,0:T(8,128)(2,1)S(1)} %get-tuple-element.37), channel_id=1, source_target_pairs={{0,3},{1,2},{2,1},{3,0},{4,7},{5,6},{6,5},{7,4},{8,11},{9,10},{10,... | collective-permute-start | bytes 196616 | tf_op jit(solution)/shard_map/ppermute | solution.py:264
  65.3 1.1 %collective-permute-done.3.refs_2_ = bf16[2,4,32,128]{3,2,1,0:T(8,128)(2,1)S(1)} collective-permute-done((bf16[2,4,32,128]{3,2,1,0:T(8,128)(2,1)S(1)}, bf16[2,4,32,128]{3,2,1,0:T(8,128)(2,1)S(1)}, u32[]{:S(2)}, u32[]{:S(2)}) %collective-permute-start.3) | collective-permute-done | bytes 65568 | tf_op jit(solution)/shard_map/ppermute | solution.py:264
  66.4 1.8 %collective-permute-done.4.refs_3_ = bf16[2,4,32,128]{3,2,1,0:T(8,128)(2,1)S(1)} collective-permute-done((bf16[2,4,32,128]{3,2,1,0:T(8,128)(2,1)S(1)}, bf16[2,4,32,128]{3,2,1,0:T(8,128)(2,1)S(1)}, u32[]{:S(2)}, u32[]{:S(2)}) %collective-permute-start.4) | collective-permute-done | bytes 65568 | tf_op jit(solution)/shard_map/ppermute | solution.py:264
  68.4 6.9 %collective-permute-start.15 = (bf16[7,32,128]{2,1,0:T(8,128)(2,1)S(1)}, bf16[7,32,128]{2,1,0:T(8,128)(2,1)S(1)}, u32[]{:S(2)}, u32[]{:S(2)}) collective-permute-start(bf16[7,32,128]{2,1,0:T(8,128)(2,1)S(1)} %get-tuple-element.50), channel_id=1, source_target_pairs={{0,4},{4,8},{8,12},{12,16},{16,20},{20,24},{24,28},{28,32},{32,36}... | collective-permute-start | bytes 172040 | tf_op jit(solution)/shard_map/ppermute | solution.py:267
  75.3 1.9 %collective-permute-start.16 = (bf16[7,32,128]{2,1,0:T(8,128)(2,1)S(1)}, bf16[7,32,128]{2,1,0:T(8,128)(2,1)S(1)}, u32[]{:S(2)}, u32[]{:S(2)}) collective-permute-start(bf16[7,32,128]{2,1,0:T(8,128)(2,1)S(1)} %get-tuple-element.51), channel_id=1, source_target_pairs={{4,0},{8,4},{12,8},{16,12},{20,16},{24,20},{28,24},{32,28},{36,32}... | collective-permute-start | bytes 172040 | tf_op jit(solution)/shard_map/ppermute | solution.py:266
  77.3 5.7 %collective-permute-done.16.from_above = bf16[7,32,128]{2,1,0:T(8,128)(2,1)S(1)} collective-permute-done((bf16[7,32,128]{2,1,0:T(8,128)(2,1)S(1)}, bf16[7,32,128]{2,1,0:T(8,128)(2,1)S(1)}, u32[]{:S(2)}, u32[]{:S(2)}) %collective-permute-start.16) | collective-permute-done | bytes 57376 | tf_op jit(solution)/shard_map/ppermute | solution.py:266
  (31 shorter events, 4.8 us)
Async XLA Ops:
  0.0 20.0 %copy-start.5 = (s32[32,8]{0,1:T(8,128)S(1)}, s32[32,8]{0,1:T(8,128)}, u32[]{:S(2)}) copy-start(s32[32,8]{0,1:T(8,128)} %param.6) | copy-start | bytes 3076
  0.0 31.0 %copy-start.4 = (s32[32]{0:T(128)S(1)}, s32[32]{0:T(128)}, u32[]{:S(2)}) copy-start(s32[32]{0:T(128)} %acount.1) | copy-start | bytes 388
  0.8 2.2 %copy-start = (bf16[32,4,128,128]{3,2,1,0:T(8,128)(2,1)S(1)}, bf16[32,4,128,128]{3,2,1,0:T(8,128)(2,1)}, u32[]{:S(2)}) copy-start(bf16[32,4,128,128]{3,2,1,0:T(8,128)(2,1)} %p_ref.1) | copy-start | bytes 12582916
  8.3 1.6 %copy-start.1 = (bf16[3,32,128,128]{3,2,1,0:T(8,128)(2,1)}, bf16[3,32,128,128]{3,2,1,0:T(8,128)(2,1)S(1)}, u32[]{:S(2)}) copy-start(bf16[3,32,128,128]{3,2,1,0:T(8,128)(2,1)S(1)} %get-tuple-element.31.pc_ref) | copy-start | bytes 9437188
  10.0 0.8 copy-start.3
  10.8 13.0 %collective-permute-start.5 = (bf16[16,128,128]{2,1,0:T(8,128)(2,1)}, bf16[16,128,128]{2,1,0:T(8,128)(2,1)S(1)}, u32[]{:S(2)}, u32[]{:S(2)}) collective-permute-start(bf16[16,128,128]{2,1,0:T(8,128)(2,1)} %get-tuple-element.38), channel_id=1, source_target_pairs={{0,1},{1,0},{2,3},{3,2},{4,5},{5,4},{6,7},{7,6},{8,9},{9,8},{10,11... | collective-permute-start | bytes 1572872 | tf_op jit(solution)/shard_map/ppermute | solution.py:255
  12.1 44.2 %collective-permute-start = (bf16[16,128,128]{2,1,0:T(8,128)(2,1)}, bf16[16,128,128]{2,1,0:T(8,128)(2,1)S(1)}, u32[]{:S(2)}, u32[]{:S(2)}) collective-permute-start(bf16[16,128,128]{2,1,0:T(8,128)(2,1)} %get-tuple-element.29), channel_id=1, source_target_pairs={{0,1},{1,0},{2,3},{3,2},{4,5},{5,4},{6,7},{7,6},{8,9},{9,8},{10,11... | collective-permute-start | bytes 1572872 | tf_op jit(solution)/shard_map/ppermute | solution.py:255
  12.2 45.7 %collective-permute-start.1 = (bf16[16,128,128]{2,1,0:T(8,128)(2,1)S(1)}, bf16[16,128,128]{2,1,0:T(8,128)(2,1)S(1)}, u32[]{:S(2)}, u32[]{:S(2)}) collective-permute-start(bf16[16,128,128]{2,1,0:T(8,128)(2,1)S(1)} %get-tuple-element.30), channel_id=1, source_target_pairs={{1,2},{3,4},{5,6},{7,8},{9,10},{11,12},{13,14},{15,16},{17,18},{19... | collective-permute-start | bytes 1572872 | tf_op jit(solution)/shard_map/ppermute | solution.py:255
  18.0 33.5 %collective-permute-start.6 = (bf16[16,128,128]{2,1,0:T(8,128)(2,1)}, bf16[16,128,128]{2,1,0:T(8,128)(2,1)S(1)}, u32[]{:S(2)}, u32[]{:S(2)}) collective-permute-start(bf16[16,128,128]{2,1,0:T(8,128)(2,1)} %get-tuple-element.39), channel_id=1, source_target_pairs={{1,2},{3,4},{5,6},{7,8},{9,10},{11,12},{13,14},{15,16},{17,18},{19... | collective-permute-start | bytes 1572872 | tf_op jit(solution)/shard_map/ppermute | solution.py:255
  19.9 32.8 %collective-permute-start.10 = (bf16[16,128,128]{2,1,0:T(8,128)(2,1)}, bf16[16,128,128]{2,1,0:T(8,128)(2,1)S(1)}, u32[]{:S(2)}, u32[]{:S(2)}) collective-permute-start(bf16[16,128,128]{2,1,0:T(8,128)(2,1)} %get-tuple-element.44), channel_id=1, source_target_pairs={{0,1},{1,0},{2,3},{3,2},{4,5},{5,4},{6,7},{7,6},{8,9},{9,8},{10,11... | collective-permute-start | bytes 1572872 | tf_op jit(solution)/shard_map/ppermute | solution.py:255
  23.8 29.2 %collective-permute-start.11 = (bf16[16,128,128]{2,1,0:T(8,128)(2,1)}, bf16[16,128,128]{2,1,0:T(8,128)(2,1)S(1)}, u32[]{:S(2)}, u32[]{:S(2)}) collective-permute-start(bf16[16,128,128]{2,1,0:T(8,128)(2,1)} %copy-done.3), channel_id=1, source_target_pairs={{1,2},{3,4},{5,6},{7,8},{9,10},{11,12},{13,14},{15,16},{17,18},{19... | collective-permute-start | bytes 1572872 | tf_op jit(solution)/shard_map/ppermute | solution.py:255
  31.0 1.9 %copy-start.2 = (bf16[3,32,128,128]{3,2,1,0:T(8,128)(2,1)S(1)}, bf16[3,32,128,128]{3,2,1,0:T(8,128)(2,1)}, u32[]{:S(2)}) copy-start(bf16[3,32,128,128]{3,2,1,0:T(8,128)(2,1)} %copy-done.1) | copy-start | bytes 9437188
  52.6 11.2 %collective-permute-start.7 = (bf16[2,4,32,128]{3,2,1,0:T(8,128)(2,1)S(1)}, bf16[2,4,32,128]{3,2,1,0:T(8,128)(2,1)S(1)}, u32[]{:S(2)}, u32[]{:S(2)}) collective-permute-start(bf16[2,4,32,128]{3,2,1,0:T(8,128)(2,1)S(1)} %get-tuple-element.41), channel_id=1, source_target_pairs={{0,1},{1,0},{2,3},{3,2},{4,5},{5,4},{6,7},{7,6},{8,9},{9,8},{10,11... | collective-permute-start | bytes 196616 | tf_op jit(solution)/shard_map/ppermute | solution.py:264
  54.0 5.9 %collective-permute-start.12 = (bf16[2,3,32,128]{3,2,1,0:T(8,128)(2,1)S(1)}, bf16[2,3,32,128]{3,2,1,0:T(8,128)(2,1)S(1)}, u32[]{:S(2)}, u32[]{:S(2)}) collective-permute-start(bf16[2,3,32,128]{3,2,1,0:T(8,128)(2,1)S(1)} %get-tuple-element.47), channel_id=1, source_target_pairs={{0,1},{1,0},{2,3},{3,2},{4,5},{5,4},{6,7},{7,6},{8,9},{9,8},{10,11... | collective-permute-start | bytes 147464 | tf_op jit(solution)/shard_map/ppermute | solution.py:264
  55.2 6.2 %collective-permute-start.13 = (bf16[2,3,32,128]{3,2,1,0:T(8,128)(2,1)S(1)}, bf16[2,3,32,128]{3,2,1,0:T(8,128)(2,1)S(1)}, u32[]{:S(2)}, u32[]{:S(2)}) collective-permute-start(bf16[2,3,32,128]{3,2,1,0:T(8,128)(2,1)S(1)} %get-tuple-element.48), channel_id=1, source_target_pairs={{0,2},{1,3},{2,0},{3,1},{4,6},{5,7},{6,4},{7,5},{8,10},{9,11},{10,... | collective-permute-start | bytes 147464 | tf_op jit(solution)/shard_map/ppermute | solution.py:264
  56.3 5.4 %collective-permute-start.14 = (bf16[2,3,32,128]{3,2,1,0:T(8,128)(2,1)S(1)}, bf16[2,3,32,128]{3,2,1,0:T(8,128)(2,1)S(1)}, u32[]{:S(2)}, u32[]{:S(2)}) collective-permute-start(bf16[2,3,32,128]{3,2,1,0:T(8,128)(2,1)S(1)} %get-tuple-element.49), channel_id=1, source_target_pairs={{0,3},{1,2},{2,1},{3,0},{4,7},{5,6},{6,5},{7,4},{8,11},{9,10},{10,... | collective-permute-start | bytes 147464 | tf_op jit(solution)/shard_map/ppermute | solution.py:264
  57.9 7.4 %collective-permute-start.8 = (bf16[2,4,32,128]{3,2,1,0:T(8,128)(2,1)S(1)}, bf16[2,4,32,128]{3,2,1,0:T(8,128)(2,1)S(1)}, u32[]{:S(2)}, u32[]{:S(2)}) collective-permute-start(bf16[2,4,32,128]{3,2,1,0:T(8,128)(2,1)S(1)} %get-tuple-element.42), channel_id=1, source_target_pairs={{0,2},{1,3},{2,0},{3,1},{4,6},{5,7},{6,4},{7,5},{8,10},{9,11},{10,... | collective-permute-start | bytes 196616 | tf_op jit(solution)/shard_map/ppermute | solution.py:264
  59.9 5.4 %collective-permute-start.9 = (bf16[2,4,32,128]{3,2,1,0:T(8,128)(2,1)S(1)}, bf16[2,4,32,128]{3,2,1,0:T(8,128)(2,1)S(1)}, u32[]{:S(2)}, u32[]{:S(2)}) collective-permute-start(bf16[2,4,32,128]{3,2,1,0:T(8,128)(2,1)S(1)} %get-tuple-element.43), channel_id=1, source_target_pairs={{0,3},{1,2},{2,1},{3,0},{4,7},{5,6},{6,5},{7,4},{8,11},{9,10},{10,... | collective-permute-start | bytes 196616 | tf_op jit(solution)/shard_map/ppermute | solution.py:264
  61.4 3.9 %collective-permute-start.2 = (bf16[2,4,32,128]{3,2,1,0:T(8,128)(2,1)S(1)}, bf16[2,4,32,128]{3,2,1,0:T(8,128)(2,1)S(1)}, u32[]{:S(2)}, u32[]{:S(2)}) collective-permute-start(bf16[2,4,32,128]{3,2,1,0:T(8,128)(2,1)S(1)} %get-tuple-element.35), channel_id=1, source_target_pairs={{0,1},{1,0},{2,3},{3,2},{4,5},{5,4},{6,7},{7,6},{8,9},{9,8},{10,11... | collective-permute-start | bytes 196616 | tf_op jit(solution)/shard_map/ppermute | solution.py:264
  61.7 4.7 %collective-permute-start.3 = (bf16[2,4,32,128]{3,2,1,0:T(8,128)(2,1)S(1)}, bf16[2,4,32,128]{3,2,1,0:T(8,128)(2,1)S(1)}, u32[]{:S(2)}, u32[]{:S(2)}) collective-permute-start(bf16[2,4,32,128]{3,2,1,0:T(8,128)(2,1)S(1)} %get-tuple-element.36), channel_id=1, source_target_pairs={{0,2},{1,3},{2,0},{3,1},{4,6},{5,7},{6,4},{7,5},{8,10},{9,11},{10,... | collective-permute-start | bytes 196616 | tf_op jit(solution)/shard_map/ppermute | solution.py:264
  63.8 4.3 %collective-permute-start.4 = (bf16[2,4,32,128]{3,2,1,0:T(8,128)(2,1)S(1)}, bf16[2,4,32,128]{3,2,1,0:T(8,128)(2,1)S(1)}, u32[]{:S(2)}, u32[]{:S(2)}) collective-permute-start(bf16[2,4,32,128]{3,2,1,0:T(8,128)(2,1)S(1)} %get-tuple-element.37), channel_id=1, source_target_pairs={{0,3},{1,2},{2,1},{3,0},{4,7},{5,6},{6,5},{7,4},{8,11},{9,10},{10,... | collective-permute-start | bytes 196616 | tf_op jit(solution)/shard_map/ppermute | solution.py:264
  68.4 8.9 %collective-permute-start.15 = (bf16[7,32,128]{2,1,0:T(8,128)(2,1)S(1)}, bf16[7,32,128]{2,1,0:T(8,128)(2,1)S(1)}, u32[]{:S(2)}, u32[]{:S(2)}) collective-permute-start(bf16[7,32,128]{2,1,0:T(8,128)(2,1)S(1)} %get-tuple-element.50), channel_id=1, source_target_pairs={{0,4},{4,8},{8,12},{12,16},{16,20},{20,24},{24,28},{28,32},{32,36}... | collective-permute-start | bytes 172040 | tf_op jit(solution)/shard_map/ppermute | solution.py:267
  75.3 7.6 %collective-permute-start.16 = (bf16[7,32,128]{2,1,0:T(8,128)(2,1)S(1)}, bf16[7,32,128]{2,1,0:T(8,128)(2,1)S(1)}, u32[]{:S(2)}, u32[]{:S(2)}) collective-permute-start(bf16[7,32,128]{2,1,0:T(8,128)(2,1)S(1)} %get-tuple-element.51), channel_id=1, source_target_pairs={{4,0},{8,4},{12,8},{16,12},{20,16},{24,20},{28,24},{32,28},{36,32}... | collective-permute-start | bytes 172040 | tf_op jit(solution)/shard_map/ppermute | solution.py:266

commit v2 on v0

v2 whole, which is shorter than its diff:
```python
import jax
import jax.numpy as jnp
from jax import lax
from jax.experimental import pallas as pl
from jax.experimental.pallas import tpu as pltpu
from jax.sharding import PartitionSpec as P

AGG = 16
TILE = 128
SLOTS_A = 8
SLOTS_P = 4
ROWS = 32
SUBS = 4
WIDE = TILE // SUBS
F32 = jnp.float32
BF16 = jnp.bfloat16
MIB = 1 << 20
STEP = 4
GROUPS = ((0, 1), (2,))
VMEM = pl.BlockSpec(memory_space=pltpu.VMEM)
SMEM = pl.BlockSpec(memory_space=pltpu.SMEM)
HBM = pl.BlockSpec(memory_space=pltpu.HBM)


def place():
    fine = lax.axis_index("fine")
    sub = lax.axis_index("sub")
    return fine * SUBS + sub, sub, lax.rem(sub, 2)


def where_of(chunk):
    for g, group in enumerate(GROUPS):
        if chunk in group:
            return g, group.index(chunk)
    raise ValueError(chunk)


def fetch(source, target, sems, first, i):
    rows = pl.ds((first + i) * STEP, STEP)
    here = pl.ds(i * STEP, STEP)
    return pltpu.make_async_copy(source.at[rows], target.at[here], sems.at[i])


def collapse_rows(group, cols, p_hbm, held, sems, by_a, by_b, half):
    device, sub, parity = place()
    agg = device * 2 + half
    steps = AGG // STEP
    part = TILE // 4

    def fill(target):
        def rows_at(i, carry):
            first = half * steps + i
            fetch(p_hbm, held, sems, 0, first).wait()
            for r in range(STEP):
                row = first * STEP + r
                rel = [cols[k, row] - agg for k in range(SLOTS_P)]
                for q in range(4):
                    lines = slice(q * part, (q + 1) * part)
                    tiles = [held[row, k, lines].astype(F32) for k in range(SLOTS_P)]
                    for at, c in enumerate(group):
                        m = 1 - c if half == 1 else c - 1
                        value = jnp.where(rel[0] == m, tiles[0], 0.0)
                        for k in range(1, SLOTS_P):
                            value = value + jnp.where(rel[k] == m, tiles[k], 0.0)
                        target[at, i * STEP + r, lines] = value.astype(BF16)
            return carry

        lax.fori_loop(0, steps, rows_at, 0)

    @pl.when(parity == 1 - half)
    def _():
        fill(by_a)

    @pl.when(parity == half)
    def _():
        fill(by_b)


def collapse_kernel(cols, p_hbm, by_a, by_b, held, sems):
    for i in range(ROWS // STEP):
        fetch(p_hbm, held, sems, 0, i).start()
    for half in range(2):
        collapse_rows(GROUPS[0], cols, p_hbm, held, sems, by_a, by_b, half)


def collapse(p_tiles, p_cols):
    shape = jax.ShapeDtypeStruct((len(GROUPS[0]), AGG, TILE, TILE), BF16)
    return pl.pallas_call(
        collapse_kernel,
        out_shape=[shape, shape],
        in_specs=[SMEM, HBM],
        out_specs=[VMEM] * 2,
        scratch_shapes=[
            pltpu.VMEM((ROWS, SLOTS_P, TILE, TILE), BF16),
            pltpu.SemaphoreType.DMA((ROWS // STEP,)),
        ],
        compiler_params=pltpu.CompilerParams(vmem_limit_bytes=48 * MIB),
        cost_estimate=pl.CostEstimate(flops=8 * MIB, bytes_accessed=6 * MIB, transcendentals=0),
    )(p_cols.T, p_tiles)


def local_rows(half, acols, acount, a_hbm, by_a, by_b, out_ref, rh_ref, total, held, pc, sems):
    device, sub, parity = place()
    base = device * ROWS + half * AGG - AGG

    def spread(i, carry):
        for c in range(3):
            g, at = where_of(c)

            @pl.when(parity == 0)
            def _():
                pc[2 - c, AGG + i] = by_a[g][at, i]
                pc[c, i] = by_b[g][at, i]

            @pl.when(parity == 1)
            def _():
                pc[c, i] = by_a[g][at, i]
                pc[2 - c, AGG + i] = by_b[g][at, i]

        total[3 * i] = jnp.zeros((3 * TILE, TILE), F32)
        total[3 * i + 1] = jnp.zeros((3 * TILE, TILE), F32)
        total[3 * i + 2] = jnp.zeros((3 * TILE, TILE), F32)
        return carry

    lax.fori_loop(0, AGG, spread, 0)

    def rows_at(i, carry):
        fetch(a_hbm, held, sems, half * (AGG // STEP), i).wait()
        for r in range(STEP):
            near = i * STEP + r
            row = half * AGG + near
            own = jnp.concatenate([pc[m, row].T for m in range(3)], axis=0)
            used = acount[row]
            for k in range(0, SLOTS_A, 2):
                pair = jnp.concatenate([held[near, k], held[near, k + 1]], axis=1)
                both = jnp.dot(own, pair, preferred_element_type=F32)
                for e in range(2):
                    at = jnp.where(k + e < used, acols[k + e, row] - base, 3 * AGG)
                    total[at] += both[:, e * TILE : (e + 1) * TILE]
        return carry

    lax.fori_loop(0, AGG // STEP, rows_at, 0)
    for c in range(AGG):
        rh_ref[half, :, c * TILE : (c + 1) * TILE] = total[2 * AGG * half + c].astype(BF16)
    for o in range(5):
        out_ref[half, o] = jnp.zeros((3 * TILE, TILE), F32)
    for b in range(2):
        first = AGG * (b - half + 1)
        left = jnp.concatenate([total[first + c].astype(BF16) for c in range(AGG)], axis=1)
        right = jnp.concatenate(
            [pc[m, AGG * b : AGG * (b + 1)].reshape(AGG * TILE, TILE) for m in range(3)],
            axis=1,
        )
        part = jnp.dot(left, right, preferred_element_type=F32)
        for m in range(3):
            out_ref[half, b - half + 1 + m] += part[:, m * TILE : (m + 1) * TILE]


def first_kernel(
    acols, acount, cols, a_hbm, p_hbm, a0, b0, a1, b1, out_ref, rh_ref, total, held, pc, p_held, sems, p_sems
):
    for i in range(ROWS // STEP):
        fetch(p_hbm, p_held, p_sems, 0, i).start()
    for i in range(AGG // STEP):
        fetch(a_hbm, held, sems, 0, i).start()
    for half in range(2):
        collapse_rows(GROUPS[1], cols, p_hbm, p_held, p_sems, a1, b1, half)
    local_rows(
        0, acols, acount, a_hbm, (a0, a1), (b0, b1), out_ref, rh_ref, total, held, pc, sems
    )


def second_kernel(
    acols, acount, a_hbm, a0, b0, a1, b1, out_in, rh_in, out_ref, rh_ref, total, held, pc, sems
):
    for i in range(AGG // STEP):
        fetch(a_hbm, held, sems, AGG // STEP, i).start()
    local_rows(
        1, acols, acount, a_hbm, (a0, a1), (b0, b1), out_ref, rh_ref, total, held, pc, sems
    )


LOCAL = [
    jax.ShapeDtypeStruct((2, 5, 3 * TILE, TILE), F32),
    jax.ShapeDtypeStruct((2, 3 * TILE, AGG * TILE), BF16),
]


def scratch():
    return [
        pltpu.VMEM((3 * AGG + 1, 3 * TILE, TILE), F32),
        pltpu.VMEM((AGG, SLOTS_A, TILE, TILE), BF16),
        pltpu.VMEM((3, ROWS, TILE, TILE), BF16),
    ]


def first_half(a_tiles, a_cols, a_count, p_tiles, p_cols, a0, b0):
    shape = jax.ShapeDtypeStruct((len(GROUPS[1]), AGG, TILE, TILE), BF16)
    return pl.pallas_call(
        first_kernel,
        out_shape=[shape, shape] + LOCAL,
        in_specs=[SMEM, SMEM, SMEM, HBM, HBM, VMEM, VMEM],
        out_specs=[VMEM] * 4,
        scratch_shapes=scratch()
        + [
            pltpu.VMEM((ROWS, SLOTS_P, TILE, TILE), BF16),
            pltpu.SemaphoreType.DMA((AGG // STEP,)),
            pltpu.SemaphoreType.DMA((ROWS // STEP,)),
        ],
        compiler_params=pltpu.CompilerParams(vmem_limit_bytes=40 * MIB),
        cost_estimate=pl.CostEstimate(
            flops=8 * 1024 * MIB, bytes_accessed=8 * MIB, transcendentals=0
        ),
    )(a_cols.T, a_count, p_cols.T, a_tiles, p_tiles, a0, b0)


def second_half(a_tiles, a_cols, a_count, a0, b0, a1, b1, local, rh):
    return pl.pallas_call(
        second_kernel,
        out_shape=LOCAL,
        in_specs=[SMEM, SMEM, HBM] + [VMEM] * 6,
        out_specs=[VMEM] * 2,
        scratch_shapes=scratch() + [pltpu.SemaphoreType.DMA((AGG // STEP,))],
        input_output_aliases={7: 0, 8: 1},
        compiler_params=pltpu.CompilerParams(vmem_limit_bytes=40 * MIB),
        cost_estimate=pl.CostEstimate(
            flops=8 * 1024 * MIB, bytes_accessed=8 * MIB, transcendentals=0
        ),
    )(a_cols.T, a_count, a_tiles, a0, b0, a1, b1, local, rh)


def tiles_of(chunk):
    return (0, 1, 2, 3) if chunk < 2 else (0, 1, 2)


def edge_tiles(group):
    below, above, at = [], [], 0
    for chunk in group:
        for t in tiles_of(chunk):
            for side in range(2):
                i = t if chunk < 2 else t + side
                column = 1 + chunk if side else -chunk
                if i == 0:
                    below.append((side, at, column + 4))
                if i == 3:
                    above.append((side, at, column + 1))
            at += 1
    below = [b for b in below if 2 <= b[2] < 7]
    above = [b for b in above if 0 <= b[2] < 5]
    return sorted(below, key=lambda b: b[2]), sorted(above, key=lambda b: b[2])


def finish_kernel(group, ha_ref, hb_ref, rh_ref, out_ref, *refs):
    tiles, edge = refs[-2:]
    device, sub, parity = place()
    for x, halo in enumerate((ha_ref, hb_ref)):
        side = x ^ (1 - parity)
        right = jnp.concatenate(
            [halo[at].reshape(AGG * TILE, TILE) for at in range(len(group))], axis=1
        )
        parts = jnp.dot(rh_ref[side], right, preferred_element_type=F32)
        first = 0
        for at, chunk in enumerate(group):
            part = parts[:, at * TILE : (at + 1) * TILE]
            part = part + out_ref[side, jnp.where(side == 0, 2 - chunk, 2 + chunk)]
            if chunk < 2:
                other = out_ref[1 - side, jnp.where(side == 0, 1 - chunk, 3 + chunk)]
                low = jnp.where(side == 0, part, other)
                high = jnp.where(side == 0, other, part)
                tiles[side, first] = low[:TILE]
                tiles[side, first + 1] = low[TILE : 2 * TILE] + high[:TILE]
                tiles[side, first + 2] = low[2 * TILE :] + high[TILE : 2 * TILE]
                tiles[side, first + 3] = high[2 * TILE :]
            else:
                for t in range(3):
                    tiles[side, first + t] = part[t * TILE : (t + 1) * TILE]
            first += len(tiles_of(chunk))
    below, above = edge_tiles(group)
    taken = edge.shape[0] - len(below)
    if taken:
        edge[:taken] = refs[0][...]

    @pl.when(sub == 0)
    def _():
        for n, (side, at, _j) in enumerate(below):
            edge[taken + n] = tiles[side, at].astype(BF16)

    @pl.when(sub == SUBS - 1)
    def _():
        for n, (side, at, _j) in enumerate(above):
            edge[taken + n] = tiles[side, at].astype(BF16)


def finish(group, ha, hb, rh, local, *before):
    count = sum(len(tiles_of(c)) for c in group)
    edges = len(edge_tiles(group)[0]) + sum(b.shape[0] for b in before)

    def kernel(*refs):
        finish_kernel(group, *refs)

    return pl.pallas_call(
        kernel,
        out_shape=[
            jax.ShapeDtypeStruct((2, count, TILE, TILE), F32),
            jax.ShapeDtypeStruct((edges, TILE, TILE), BF16),
        ],
        in_specs=[VMEM] * (4 + len(before)),
        out_specs=[VMEM] * 2,
        compiler_params=pltpu.CompilerParams(vmem_limit_bytes=24 * MIB),
        cost_estimate=pl.CostEstimate(
            flops=400 * MIB, bytes_accessed=6 * MIB, transcendentals=0
        ),
    )(ha, hb, rh, local, *before)


def split_kernel(tiles0, tiles1, edge, mine, to1, to2, to3):
    device, sub, parity = place()
    for d, target in enumerate((mine, to1, to2, to3)):
        rows = pl.ds(pl.multiple_of((sub ^ d) * WIDE, WIDE), WIDE)
        base, taken = 0, 0
        for group, tiles in zip(GROUPS, (tiles0, tiles1), strict=True):
            below, above = edge_tiles(group)
            for side in range(2):
                for i in range(tiles.shape[1]):
                    target[side, base + i] = tiles[side, i, rows, :].astype(BF16)

            @pl.when(sub == 0)
            def _():
                for n, (side, at, _j) in enumerate(below):
                    target[side, base + at] = edge[taken + n, rows, :]

            @pl.when(sub == SUBS - 1)
            def _():
                for n, (side, at, _j) in enumerate(above):
                    target[side, base + at] = edge[taken + n, rows, :]

            base += tiles.shape[1]
            taken += len(below)


def split(tiles, edge):
    count = sum(t.shape[1] for t in tiles)
    shape = jax.ShapeDtypeStruct((2, count, WIDE, TILE), BF16)
    return pl.pallas_call(
        split_kernel,
        out_shape=[shape] * SUBS,
        in_specs=[VMEM] * 3,
        out_specs=[VMEM] * SUBS,
        compiler_params=pltpu.CompilerParams(vmem_limit_bytes=16 * MIB),
    )(*tiles, edge)


def gather_kernel(*refs):
    parts = refs[:4]
    out_ref, window = refs[4:]
    device, sub, parity = place()
    window[...] = jnp.zeros_like(window)
    for d in range(4):
        part = parts[d]
        first = 2 * (sub ^ d)
        at = 0
        for group in GROUPS:
            for chunk in group:
                for t in tiles_of(chunk):
                    for side in range(2):
                        column = 1 + chunk if side else -chunk
                        i = t if chunk < 2 else t + side
                        if 0 <= column - i + 4 < 7:
                            row = first + i - 1
                            row = jnp.where(row < 0, 7, jnp.where(row > 7, 0, row))
                            window[row, column - i + 4] += part[side, at].astype(F32)
                    at += 1
    out_ref[...] = window[...]


def gather_parts(parts):
    return pl.pallas_call(
        gather_kernel,
        out_shape=jax.ShapeDtypeStruct((8, 7, WIDE, TILE), F32),
        in_specs=[VMEM] * len(parts),
        out_specs=VMEM,
        scratch_shapes=[pltpu.VMEM((8, 7, WIDE, TILE), F32)],
        compiler_params=pltpu.CompilerParams(vmem_limit_bytes=16 * MIB),
    )(*parts)


def shards(a_tiles, a_cols, a_count, p_tiles, p_cols):
    fines = lax.axis_size("fine")
    total = fines * SUBS
    both = ("fine", "sub")
    pairs_a = [(i, i ^ 1) for i in range(total)]
    pairs_b = [(i, (i - 1 + 2 * (i % 2)) % total) for i in range(total)]
    hop = []
    for f in range(fines):
        for q in range(SUBS):
            other = f - 1 if q < SUBS // 2 else f + 1
            hop.append((f * SUBS + q, other % fines * SUBS + q))

    a0, b0 = collapse(p_tiles, p_cols)
    halo = [(lax.ppermute(a0, both, pairs_a), lax.ppermute(b0, both, pairs_b))]
    a1, b1, local, rh = first_half(a_tiles, a_cols, a_count, p_tiles, p_cols, a0, b0)
    halo.append((lax.ppermute(a1, both, pairs_a), lax.ppermute(b1, both, pairs_b)))
    local, rh = second_half(a_tiles, a_cols, a_count, a0, b0, a1, b1, local, rh)
    tiles, edges = [], []
    for group, (ha, hb) in zip(GROUPS, halo, strict=True):
        done, edge = finish(group, ha, hb, rh, local, *edges)
        tiles.append(done)
        edges = [edge]
    parts = list(split(tiles, lax.ppermute(edges[0], both, hop)))
    for d in range(1, SUBS):
        route = [(i, i ^ d) for i in range(SUBS)]
        parts[d] = lax.ppermute(parts[d], "sub", route)
    return gather_parts(parts)


def solution(mesh):
    in_specs = (
        P(("fine", "sub"), None, None, None),
        P(("fine", "sub"), None),
        P(("fine", "sub")),
        P(("fine", "sub"), None, None, None),
        P(("fine", "sub"), None),
    )
    out_specs = P("fine", None, "sub", None)
    return jax.shard_map(shards, mesh=mesh, in_specs=in_specs, out_specs=out_specs, check_vma=False)
```

time: 596 us -> 65.9 us (0.11); the launches traced: 586 us -> 64.8 us
  local copies, waits for them, and re-layouts: 270 us -> 0.85 us
  matrix products: 150 us -> 0 us
  waiting for transfers between devices: 91.6 us -> 22.6 us
  other arithmetic: 37.9 us -> 0 us
  Pallas kernels: 0 us -> 26.6 us
  between operations: 13.5 us -> 0.07 us
  starting transfers between devices: 20.9 us -> 14.7 us
    dot_general x48 -> x0, matrix products: 150 us -> none  [the longest x16 85.6 us: step(): jnp.einsum('gkmo,gkamc->goac', picker, products, precision=highest)]
    reshape x17 -> x0, local copies, waits for them, and re-layouts: 84.2 us -> none  [the longest x16 84.2 us: step(): products.reshape(products.shape[0], products.shape[1], tile_size, slot_to...]
    gather x48 -> x0, local copies, waits for them, and re-layouts: 75.4 us -> none  [the longest x16 65 us: step(): fetched = ext_wide[local_rows]]
    reduce_scatter x1 -> x0, waiting for transfers between devices: 52.4 us -> none  [shards(): lax.psum_scatter(partial_value, 'sub', scatter_dimension=2, tiled=True)]
    dynamic_slice x32 -> x0, local copies, waits for them, and re-layouts: 29.9 us -> none  [step(): current = lax.dynamic_slice_in_dim(total, start, 3, 0)]
    another operation x32 -> x0, local copies, waits for them, and re-layouts: 26.6 us -> none  [step(): contrib = jnp.stack(placed)]
    pallas_call x0 -> x7, Pallas kernels: none -> 26.6 us  [the longest x1 10.6 us: first_half(): pl.pallas_call(first_kernel, out_shape=[shape, shape] + LOCAL, in_specs=[...]
    dynamic_update_slice x32 -> x0, local copies, waits for them, and re-layouts: 26.4 us -> none  [step(): total = lax.dynamic_update_slice_in_dim(total, current + contrib, start, 0)]
  transfers between devices with their start and end apart: 7 -> 8, of which waited for: 5 -> 5; matrix products, arithmetic and copies ran while one was open for 0% -> 0% of each run, Pallas kernels for 0% -> 33%
where the time goes in v2:
time: 65.9 us; the launch traced here: 64.8 us
  Pallas kernels  26.6 us (40%)
  waiting for transfers between devices  22.6 us (34%)
  starting transfers between devices  14.7 us (22%)
  local copies, waits for them, and re-layouts  0.85 us (1%)
    pallas_call x1, Pallas kernels, first_half(): pl.pallas_call(first_kernel, out_shape=[shape, shape] + LOCAL, in_specs=[...  10.6 us
    ppermute x3, waiting for transfers between devices, shards(): parts[d] = lax.ppermute(parts[d], 'sub', route)  10.4 us
    pallas_call x1, Pallas kernels, second_half(): pl.pallas_call(second_kernel, out_shape=LOCAL, in_specs=[SMEM, SMEM, HBM]...  9.39 us
    ppermute x1, waiting for transfers between devices, shards(): lax.ppermute(a1, both, pairs_a)  8.97 us
    ppermute x3, starting transfers between devices, shards(): parts[d] = lax.ppermute(parts[d], 'sub', route)  5.62 us
    ppermute x1, starting transfers between devices, shards(): parts = list(split(tiles, lax.ppermute(edges[0], both, hop)))  3.4 us
    ppermute x2, starting transfers between devices, shards(): halo = [(lax.ppermute(a0, both, pairs_a), lax.ppermute(b0, both, pairs_b))]  3.26 us
    pallas_call x1, Pallas kernels, collapse(): pl.pallas_call(collapse_kernel, out_shape=[shape, shape], in_specs=[SMEM,...  3.11 us
  transfers between devices with their start and end apart: 8, of which 5 were waited for; matrix products, arithmetic and copies ran while one was open for 0% of the time, Pallas kernels for 33%

profile of v2, /device:TPU:38, one launch (start us, length us, event | category | flops | bytes accessed | tf_op | source)
XLA Modules:
  0.0 64.8 jit_solution(15250439816304383012)
XLA Ops:
  0.0 0.8 %copy-done.1 = s32[32,4]{0,1:T(4,128)S(1)} copy-done((s32[32,4]{0,1:T(4,128)S(1)}, s32[32,4]{0,1:T(4,128)}, u32[]{:S(2)}) %copy-start.1) | copy-done | bytes 536
  0.8 3.1 %shard_map.55 = (bf16[2,16,128,128]{3,2,1,0:T(8,128)(2,1)S(1)}, bf16[2,16,128,128]{3,2,1,0:T(8,128)(2,1)S(1)}) custom-call(s32[4,32]{1,0:T(4,128)S(1)} %bitcast.2, bf16[32,4,128,128]{3,2,1,0:T(8,128)(2,1)} %p_hbm.3), custom_call_target="tpu_custom_call" | custom-call | flops 8388608 | bytes 6291456 | tf_op jit(solution)/shard_map/pallas_call | solution.py:88
  4.0 1.7 %collective-permute-start = (bf16[2,16,128,128]{3,2,1,0:T(8,128)(2,1)S(1)}, bf16[2,16,128,128]{3,2,1,0:T(8,128)(2,1)S(1)}, u32[]{:S(2)}, u32[]{:S(2)}) collective-permute-start(bf16[2,16,128,128]{3,2,1,0:T(8,128)(2,1)S(1)} %get-tuple-element.21.a0), channel_id=1, source_target_pairs={{0,1},{1,0},{2,3},{3,2},{4,5},{5,4},{6,7},{7,6},{8,9},{9,8},{10,11... | collective-permute-start | bytes 3145736 | tf_op jit(solution)/shard_map/ppermute | solution.py:400
  5.6 1.6 %collective-permute-start.1 = (bf16[2,16,128,128]{3,2,1,0:T(8,128)(2,1)S(1)}, bf16[2,16,128,128]{3,2,1,0:T(8,128)(2,1)S(1)}, u32[]{:S(2)}, u32[]{:S(2)}) collective-permute-start(bf16[2,16,128,128]{3,2,1,0:T(8,128)(2,1)S(1)} %get-tuple-element.22.b0), channel_id=1, source_target_pairs={{0,127},{1,2},{2,1},{3,4},{4,3},{5,6},{6,5},{7,8},{8,7},{9,10},{10... | collective-permute-start | bytes 3145736 | tf_op jit(solution)/shard_map/ppermute | solution.py:400
  7.2 10.6 %shard_map.56 = (bf16[1,16,128,128]{3,2,1,0:T(8,128)(2,1)S(1)}, bf16[1,16,128,128]{3,2,1,0:T(8,128)(2,1)S(1)}, f32[2,5,384,128]{3,2,1,0:T(8,128)S(1)}, bf16[2,384,2048]{2,1,0:T(8,128)(2,1)S(1)}) custom-call(s32[8,32]{1,0:T(8,128)S(1)} %bitcast.4, s32[32]{0:T(128)S(1)} %copy-done.4, s32[4,32]{1,0:T(4,128)S(1)} %bitcast.3, bf16[32,8,128,128]{3,2,1,0:T(8,128)(2,1)} %a_hbm.3, ...), custom_call_target="tpu_custom_call" | custom-call | flops 8589934592 | bytes 8388608 | tf_op jit(solution)/shard_map/pallas_call | solution.py:199
  17.9 1.3 %collective-permute-start.2 = (bf16[1,16,128,128]{3,2,1,0:T(8,128)(2,1)S(1)}, bf16[1,16,128,128]{3,2,1,0:T(8,128)(2,1)S(1)}, u32[]{:S(2)}, u32[]{:S(2)}) collective-permute-start(bf16[1,16,128,128]{3,2,1,0:T(8,128)(2,1)S(1)} %get-tuple-element.23.a1), channel_id=1, source_target_pairs={{0,1},{1,0},{2,3},{3,2},{4,5},{5,4},{6,7},{7,6},{8,9},{9,8},{10,11... | collective-permute-start | bytes 1572872 | tf_op jit(solution)/shard_map/ppermute | solution.py:402
  19.2 1.1 %collective-permute-start.3 = (bf16[1,16,128,128]{3,2,1,0:T(8,128)(2,1)S(1)}, bf16[1,16,128,128]{3,2,1,0:T(8,128)(2,1)S(1)}, u32[]{:S(2)}, u32[]{:S(2)}) collective-permute-start(bf16[1,16,128,128]{3,2,1,0:T(8,128)(2,1)S(1)} %get-tuple-element.24.b1), channel_id=1, source_target_pairs={{0,127},{1,2},{2,1},{3,4},{4,3},{5,6},{6,5},{7,8},{8,7},{9,10},{10... | collective-permute-start | bytes 1572872 | tf_op jit(solution)/shard_map/ppermute | solution.py:402
  20.3 9.4 %shard_map.57 = (f32[2,5,384,128]{3,2,1,0:T(8,128)S(1)}, bf16[2,384,2048]{2,1,0:T(8,128)(2,1)S(1)}) custom-call(s32[8,32]{1,0:T(8,128)S(1)} %bitcast.5, s32[32]{0:T(128)S(1)} %copy-done.4, bf16[32,8,128,128]{3,2,1,0:T(8,128)(2,1)} %a_hbm.3, bf16[2,16,128,128]{3,2,1,0:T(8,128)(2,1)S(1)} %get-tuple-element.21.a0, ...), custom_call_target="tpu_custom_call", output_to_operand_aliasing={{0}: (7, {}), {1}: (8, {})} | custom-call | flops 8589934592 | bytes 8388608 | tf_op jit(solution)/shard_map/pallas_call | solution.py:218
  29.7 0.4 collective-permute-done.refs_0_
  30.1 0.0 collective-permute-done.1.refs_1_
  30.1 1.1 %shard_map.58 = (f32[2,8,128,128]{3,2,1,0:T(8,128)S(1)}, bf16[4,128,128]{2,1,0:T(8,128)(2,1)S(1)}) custom-call(bf16[2,16,128,128]{3,2,1,0:T(8,128)(2,1)S(1)} %collective-permute-done.refs_0_, bf16[2,16,128,128]{3,2,1,0:T(8,128)(2,1)S(1)} %collective-permute-done.1.refs_1_, bf16[2,384,2048]{2,1,0:T(8,128)(2,1)S(1)} %get-tuple-element.27.refs_2_, ...), custom_call_target="tpu_custom_call" | custom-call | flops 419430400 | bytes 6291456 | tf_op jit(solution)/shard_map/pallas_call | solution.py:301
  31.2 9.0 %collective-permute-done.2.refs_0_ = bf16[1,16,128,128]{3,2,1,0:T(8,128)(2,1)S(1)} collective-permute-done((bf16[1,16,128,128]{3,2,1,0:T(8,128)(2,1)S(1)}, bf16[1,16,128,128]{3,2,1,0:T(8,128)(2,1)S(1)}, u32[]{:S(2)}, u32[]{:S(2)}) %collective-permute-start.2) | collective-permute-done | bytes 524320 | tf_op jit(solution)/shard_map/ppermute | solution.py:402
  40.2 0.0 collective-permute-done.3.refs_1_
  40.2 1.0 %shard_map.59 = (f32[2,3,128,128]{3,2,1,0:T(8,128)S(1)}, bf16[5,128,128]{2,1,0:T(8,128)(2,1)S(1)}) custom-call(bf16[1,16,128,128]{3,2,1,0:T(8,128)(2,1)S(1)} %collective-permute-done.2.refs_0_, bf16[1,16,128,128]{3,2,1,0:T(8,128)(2,1)S(1)} %collective-permute-done.3.refs_1_, bf16[2,384,2048]{2,1,0:T(8,128)(2,1)S(1)} %get-tuple-element.27.refs_2_, ...), custom_call_target="tpu_custom_call" | custom-call | flops 419430400 | bytes 6291456 | tf_op jit(solution)/shard_map/pallas_call | solution.py:301
  41.2 3.4 %collective-permute-start.4 = (bf16[5,128,128]{2,1,0:T(8,128)(2,1)S(1)}, bf16[5,128,128]{2,1,0:T(8,128)(2,1)S(1)}, u32[]{:S(2)}, u32[]{:S(2)}) collective-permute-start(bf16[5,128,128]{2,1,0:T(8,128)(2,1)S(1)} %get-tuple-element.32), channel_id=1, source_target_pairs={{0,124},{1,125},{2,6},{3,7},{4,0},{5,1},{6,10},{7,11},{8,4},{9,5},... | collective-permute-start | bytes 491528 | tf_op jit(solution)/shard_map/ppermute | solution.py:409
  44.6 2.8 %collective-permute-done.4.edge = bf16[5,128,128]{2,1,0:T(8,128)(2,1)S(1)} collective-permute-done((bf16[5,128,128]{2,1,0:T(8,128)(2,1)S(1)}, bf16[5,128,128]{2,1,0:T(8,128)(2,1)S(1)}, u32[]{:S(2)}, u32[]{:S(2)}) %collective-permute-start.4) | collective-permute-done | bytes 163872 | tf_op jit(solution)/shard_map/ppermute | solution.py:409
  47.4 0.1 shard_map.60
  47.6 0.1 collective-permute-start.5
  47.6 5.5 %collective-permute-start.6 = (bf16[2,11,32,128]{3,2,1,0:T(8,128)(2,1)S(1)}, bf16[2,11,32,128]{3,2,1,0:T(8,128)(2,1)S(1)}, u32[]{:S(2)}, u32[]{:S(2)}) collective-permute-start(bf16[2,11,32,128]{3,2,1,0:T(8,128)(2,1)S(1)} %get-tuple-element.35), channel_id=1, source_target_pairs={{0,2},{1,3},{2,0},{3,1},{4,6},{5,7},{6,4},{7,5},{8,10},{9,11},{10,... | collective-permute-start | bytes 540680 | tf_op jit(solution)/shard_map/ppermute | solution.py:412
  53.2 0.0 collective-permute-start.7
  53.2 0.0 collective-permute-done.5.refs_1_
  53.2 7.9 %collective-permute-done.6.refs_2_ = bf16[2,11,32,128]{3,2,1,0:T(8,128)(2,1)S(1)} collective-permute-done((bf16[2,11,32,128]{3,2,1,0:T(8,128)(2,1)S(1)}, bf16[2,11,32,128]{3,2,1,0:T(8,128)(2,1)S(1)}, u32[]{:S(2)}, u32[]{:S(2)}) %collective-permute-start.6) | collective-permute-done | bytes 180256 | tf_op jit(solution)/shard_map/ppermute | solution.py:412
  61.1 2.5 %collective-permute-done.7.refs_3_ = bf16[2,11,32,128]{3,2,1,0:T(8,128)(2,1)S(1)} collective-permute-done((bf16[2,11,32,128]{3,2,1,0:T(8,128)(2,1)S(1)}, bf16[2,11,32,128]{3,2,1,0:T(8,128)(2,1)S(1)}, u32[]{:S(2)}, u32[]{:S(2)}) %collective-permute-start.7) | collective-permute-done | bytes 180256 | tf_op jit(solution)/shard_map/ppermute | solution.py:412
  63.6 1.2 %shard_map.61 = f32[8,7,32,128]{3,2,1,0:T(8,128)} custom-call(bf16[2,11,32,128]{3,2,1,0:T(8,128)(2,1)S(1)} %get-tuple-element.33.refs_0_, bf16[2,11,32,128]{3,2,1,0:T(8,128)(2,1)S(1)} %collective-permute-done.5.refs_1_, bf16[2,11,32,128]{3,2,1,0:T(8,128)(2,1)S(1)} %collective-permute-done.6.refs_2_, bf16[2,11,32,128]{3,2,1,0:T(8,128)(2,1)S(1)} %collective-permute-done.7.refs_3_), custom_call_target="tpu_custom_call" | custom-call | tf_op jit(solution)/shard_map/pallas_call | solution.py:377
  (9 shorter events, 0.0 us)
Async XLA Ops:
  0.0 7.2 %copy-start = (bf16[32,4,128,128]{3,2,1,0:T(8,128)(2,1)S(1)}, bf16[32,4,128,128]{3,2,1,0:T(8,128)(2,1)}, u32[]{:S(2)}) copy-start(bf16[32,4,128,128]{3,2,1,0:T(8,128)(2,1)} %p_hbm.3) | copy-start | bytes 12582916
  0.0 0.8 %copy-start.1 = (s32[32,4]{0,1:T(4,128)S(1)}, s32[32,4]{0,1:T(4,128)}, u32[]{:S(2)}) copy-start(s32[32,4]{0,1:T(4,128)} %param.9) | copy-start | bytes 1540
  0.8 6.4 %copy-start.2 = (s32[32,4]{0,1:T(4,128)S(1)}, s32[32,4]{0,1:T(4,128)}, u32[]{:S(2)}) copy-start(s32[32,4]{0,1:T(4,128)} %param.9) | copy-start | bytes 1540
  0.8 6.4 %copy-start.3 = (s32[32,8]{0,1:T(8,128)S(1)}, s32[32,8]{0,1:T(8,128)}, u32[]{:S(2)}) copy-start(s32[32,8]{0,1:T(8,128)} %param.6) | copy-start | bytes 3076
  0.8 6.4 %copy-start.4 = (s32[32]{0:T(128)S(1)}, s32[32]{0:T(128)}, u32[]{:S(2)}) copy-start(s32[32]{0:T(128)} %acount.3) | copy-start | bytes 388
  4.0 26.1 %collective-permute-start = (bf16[2,16,128,128]{3,2,1,0:T(8,128)(2,1)S(1)}, bf16[2,16,128,128]{3,2,1,0:T(8,128)(2,1)S(1)}, u32[]{:S(2)}, u32[]{:S(2)}) collective-permute-start(bf16[2,16,128,128]{3,2,1,0:T(8,128)(2,1)S(1)} %get-tuple-element.21.a0), channel_id=1, source_target_pairs={{0,1},{1,0},{2,3},{3,2},{4,5},{5,4},{6,7},{7,6},{8,9},{9,8},{10,11... | collective-permute-start | bytes 3145736 | tf_op jit(solution)/shard_map/ppermute | solution.py:400
  5.6 24.5 %collective-permute-start.1 = (bf16[2,16,128,128]{3,2,1,0:T(8,128)(2,1)S(1)}, bf16[2,16,128,128]{3,2,1,0:T(8,128)(2,1)S(1)}, u32[]{:S(2)}, u32[]{:S(2)}) collective-permute-start(bf16[2,16,128,128]{3,2,1,0:T(8,128)(2,1)S(1)} %get-tuple-element.22.b0), channel_id=1, source_target_pairs={{0,127},{1,2},{2,1},{3,4},{4,3},{5,6},{6,5},{7,8},{8,7},{9,10},{10... | collective-permute-start | bytes 3145736 | tf_op jit(solution)/shard_map/ppermute | solution.py:400
  17.9 22.3 %collective-permute-start.2 = (bf16[1,16,128,128]{3,2,1,0:T(8,128)(2,1)S(1)}, bf16[1,16,128,128]{3,2,1,0:T(8,128)(2,1)S(1)}, u32[]{:S(2)}, u32[]{:S(2)}) collective-permute-start(bf16[1,16,128,128]{3,2,1,0:T(8,128)(2,1)S(1)} %get-tuple-element.23.a1), channel_id=1, source_target_pairs={{0,1},{1,0},{2,3},{3,2},{4,5},{5,4},{6,7},{7,6},{8,9},{9,8},{10,11... | collective-permute-start | bytes 1572872 | tf_op jit(solution)/shard_map/ppermute | solution.py:402
  19.2 21.0 %collective-permute-start.3 = (bf16[1,16,128,128]{3,2,1,0:T(8,128)(2,1)S(1)}, bf16[1,16,128,128]{3,2,1,0:T(8,128)(2,1)S(1)}, u32[]{:S(2)}, u32[]{:S(2)}) collective-permute-start(bf16[1,16,128,128]{3,2,1,0:T(8,128)(2,1)S(1)} %get-tuple-element.24.b1), channel_id=1, source_target_pairs={{0,127},{1,2},{2,1},{3,4},{4,3},{5,6},{6,5},{7,8},{8,7},{9,10},{10... | collective-permute-start | bytes 1572872 | tf_op jit(solution)/shard_map/ppermute | solution.py:402
  41.2 6.2 %collective-permute-start.4 = (bf16[5,128,128]{2,1,0:T(8,128)(2,1)S(1)}, bf16[5,128,128]{2,1,0:T(8,128)(2,1)S(1)}, u32[]{:S(2)}, u32[]{:S(2)}) collective-permute-start(bf16[5,128,128]{2,1,0:T(8,128)(2,1)S(1)} %get-tuple-element.32), channel_id=1, source_target_pairs={{0,124},{1,125},{2,6},{3,7},{4,0},{5,1},{6,10},{7,11},{8,4},{9,5},... | collective-permute-start | bytes 491528 | tf_op jit(solution)/shard_map/ppermute | solution.py:409
  47.6 5.6 %collective-permute-start.5 = (bf16[2,11,32,128]{3,2,1,0:T(8,128)(2,1)S(1)}, bf16[2,11,32,128]{3,2,1,0:T(8,128)(2,1)S(1)}, u32[]{:S(2)}, u32[]{:S(2)}) collective-permute-start(bf16[2,11,32,128]{3,2,1,0:T(8,128)(2,1)S(1)} %get-tuple-element.34), channel_id=1, source_target_pairs={{0,1},{1,0},{2,3},{3,2},{4,5},{5,4},{6,7},{7,6},{8,9},{9,8},{10,11... | collective-permute-start | bytes 540680 | tf_op jit(solution)/shard_map/ppermute | solution.py:412
  47.6 13.4 %collective-permute-start.6 = (bf16[2,11,32,128]{3,2,1,0:T(8,128)(2,1)S(1)}, bf16[2,11,32,128]{3,2,1,0:T(8,128)(2,1)S(1)}, u32[]{:S(2)}, u32[]{:S(2)}) collective-permute-start(bf16[2,11,32,128]{3,2,1,0:T(8,128)(2,1)S(1)} %get-tuple-element.35), channel_id=1, source_target_pairs={{0,2},{1,3},{2,0},{3,1},{4,6},{5,7},{6,4},{7,5},{8,10},{9,11},{10,... | collective-permute-start | bytes 540680 | tf_op jit(solution)/shard_map/ppermute | solution.py:412
  53.2 10.4 %collective-permute-start.7 = (bf16[2,11,32,128]{3,2,1,0:T(8,128)(2,1)S(1)}, bf16[2,11,32,128]{3,2,1,0:T(8,128)(2,1)S(1)}, u32[]{:S(2)}, u32[]{:S(2)}) collective-permute-start(bf16[2,11,32,128]{3,2,1,0:T(8,128)(2,1)S(1)} %get-tuple-element.36), channel_id=1, source_target_pairs={{0,3},{1,2},{2,1},{3,0},{4,7},{5,6},{6,5},{7,4},{8,11},{9,10},{10,... | collective-permute-start | bytes 540680 | tf_op jit(solution)/shard_map/ppermute | solution.py:412

commit v3 on v2

--- a/solution.py
+++ b/solution.py
@@ -17,6 +17,7 @@
 MIB = 1 << 20
 STEP = 4
 GROUPS = ((0, 1), (2,))
+PLAN = (((0,), (0, 1, 3)), ((1,), (0, 1, 3)), ((0, 1), (2,)))
 VMEM = pl.BlockSpec(memory_space=pltpu.VMEM)
 SMEM = pl.BlockSpec(memory_space=pltpu.SMEM)
 HBM = pl.BlockSpec(memory_space=pltpu.HBM)
@@ -250,8 +251,7 @@
     return sorted(below, key=lambda b: b[2]), sorted(above, key=lambda b: b[2])
 
 
-def finish_kernel(group, ha_ref, hb_ref, rh_ref, out_ref, *refs):
-    tiles, edge = refs[-2:]
+def finish_kernel(group, ha_ref, hb_ref, rh_ref, out_ref, tiles, edge):
     device, sub, parity = place()
     for x, halo in enumerate((ha_ref, hb_ref)):
         side = x ^ (1 - parity)
@@ -276,24 +276,21 @@
                     tiles[side, first + t] = part[t * TILE : (t + 1) * TILE]
             first += len(tiles_of(chunk))
     below, above = edge_tiles(group)
-    taken = edge.shape[0] - len(below)
-    if taken:
-        edge[:taken] = refs[0][...]
 
     @pl.when(sub == 0)
     def _():
         for n, (side, at, _j) in enumerate(below):
-            edge[taken + n] = tiles[side, at].astype(BF16)
+            edge[n] = tiles[side, at].astype(BF16)
 
     @pl.when(sub == SUBS - 1)
     def _():
         for n, (side, at, _j) in enumerate(above):
-            edge[taken + n] = tiles[side, at].astype(BF16)
-
-
-def finish(group, ha, hb, rh, local, *before):
+            edge[n] = tiles[side, at].astype(BF16)
+
+
+def finish(group, ha, hb, rh, local):
     count = sum(len(tiles_of(c)) for c in group)
-    edges = len(edge_tiles(group)[0]) + sum(b.shape[0] for b in before)
+    edges = len(edge_tiles(group)[0])
 
     def kernel(*refs):
         finish_kernel(group, *refs)
@@ -304,22 +301,24 @@
             jax.ShapeDtypeStruct((2, count, TILE, TILE), F32),
             jax.ShapeDtypeStruct((edges, TILE, TILE), BF16),
         ],
-        in_specs=[VMEM] * (4 + len(before)),
+        in_specs=[VMEM] * 4,
         out_specs=[VMEM] * 2,
         compiler_params=pltpu.CompilerParams(vmem_limit_bytes=24 * MIB),
         cost_estimate=pl.CostEstimate(
             flops=400 * MIB, bytes_accessed=6 * MIB, transcendentals=0
         ),
-    )(ha, hb, rh, local, *before)
-
-
-def split_kernel(tiles0, tiles1, edge, mine, to1, to2, to3):
+    )(ha, hb, rh, local)
+
+
+def split_kernel(groups, which, *refs):
     device, sub, parity = place()
-    for d, target in enumerate((mine, to1, to2, to3)):
+    last = device >= (lax.axis_size("fine") - 1) * SUBS
+    for d, target in zip(which, refs[2 * len(groups) :], strict=True):
         rows = pl.ds(pl.multiple_of((sub ^ d) * WIDE, WIDE), WIDE)
-        base, taken = 0, 0
-        for group, tiles in zip(GROUPS, (tiles0, tiles1), strict=True):
-            below, above = edge_tiles(group)
+        base = 0
+        for n_group, g in enumerate(groups):
+            tiles, edge = refs[2 * n_group : 2 * n_group + 2]
+            below, above = edge_tiles(GROUPS[g])
             for side in range(2):
                 for i in range(tiles.shape[1]):
                     target[side, base + i] = tiles[side, i, rows, :].astype(BF16)
@@ -327,55 +326,61 @@
             @pl.when(sub == 0)
             def _():
                 for n, (side, at, _j) in enumerate(below):
-                    target[side, base + at] = edge[taken + n, rows, :]
+                    kept = jnp.where(last, 0.0, edge[n, rows, :].astype(F32))
+                    target[side, base + at] = kept.astype(BF16)
 
             @pl.when(sub == SUBS - 1)
             def _():
                 for n, (side, at, _j) in enumerate(above):
-                    target[side, base + at] = edge[taken + n, rows, :]
+                    kept = jnp.where(device < SUBS, 0.0, edge[n, rows, :].astype(F32))
+                    target[side, base + at] = kept.astype(BF16)
 
             base += tiles.shape[1]
-            taken += len(below)
-
-
-def split(tiles, edge):
-    count = sum(t.shape[1] for t in tiles)
+
+
+def split(groups, which, tiles, edges):
+    count = sum(tiles[g].shape[1] for g in groups)
     shape = jax.ShapeDtypeStruct((2, count, WIDE, TILE), BF16)
-    return pl.pallas_call(
-        split_kernel,
-        out_shape=[shape] * SUBS,
-        in_specs=[VMEM] * 3,
-        out_specs=[VMEM] * SUBS,
+
+    def kernel(*refs):
+        split_kernel(groups, which, *refs)
+
+    return pl.pallas_call(
+        kernel,
+        out_shape=[shape] * len(which),
+        in_specs=[VMEM] * (2 * len(groups)),
+        out_specs=[VMEM] * len(which),
         compiler_params=pltpu.CompilerParams(vmem_limit_bytes=16 * MIB),
-    )(*tiles, edge)
-
-
-def gather_kernel(*refs):
-    parts = refs[:4]
-    out_ref, window = refs[4:]
+    )(*[x for g in groups for x in (tiles[g], edges[g])])
+
+
+def gather_kernel(kinds, *refs):
+    parts = refs[: len(kinds)]
+    out_ref, window = refs[len(kinds) :]
     device, sub, parity = place()
     window[...] = jnp.zeros_like(window)
-    for d in range(4):
-        part = parts[d]
+    for (d, groups), part in zip(kinds, parts, strict=True):
         first = 2 * (sub ^ d)
         at = 0
-        for group in GROUPS:
-            for chunk in group:
-                for t in tiles_of(chunk):
-                    for side in range(2):
-                        column = 1 + chunk if side else -chunk
-                        i = t if chunk < 2 else t + side
-                        if 0 <= column - i + 4 < 7:
-                            row = first + i - 1
-                            row = jnp.where(row < 0, 7, jnp.where(row > 7, 0, row))
-                            window[row, column - i + 4] += part[side, at].astype(F32)
-                    at += 1
+        for chunk in [c for g in groups for c in GROUPS[g]]:
+            for t in tiles_of(chunk):
+                for side in range(2):
+                    column = 1 + chunk if side else -chunk
+                    i = t if chunk < 2 else t + side
+                    if 0 <= column - i + 4 < 7:
+                        row = first + i - 1
+                        row = jnp.where(row < 0, 7, jnp.where(row > 7, 0, row))
+                        window[row, column - i + 4] += part[side, at].astype(F32)
+                at += 1
     out_ref[...] = window[...]
 
 
-def gather_parts(parts):
-    return pl.pallas_call(
-        gather_kernel,
+def gather_parts(kinds, parts):
+    def kernel(*refs):
+        gather_kernel(kinds, *refs)
+
+    return pl.pallas_call(
+        kernel,
         out_shape=jax.ShapeDtypeStruct((8, 7, WIDE, TILE), F32),
         in_specs=[VMEM] * len(parts),
         out_specs=VMEM,
@@ -391,26 +396,28 @@
     pairs_a = [(i, i ^ 1) for i in range(total)]
     pairs_b = [(i, (i - 1 + 2 * (i % 2)) % total) for i in range(total)]
     hop = []
-    for f in range(fines):
-        for q in range(SUBS):
-            other = f - 1 if q < SUBS // 2 else f + 1
-            hop.append((f * SUBS + q, other % fines * SUBS + q))
+    for q, other, step in ((0, 1, -1), (3, 2, 1)):
+        down = [f * SUBS + q for f in range(fines)][::step]
+        back = [f * SUBS + other for f in range(fines)][::-step]
+        loop = down + back
+        hop += list(zip(loop, loop[1:] + loop[:1], strict=True))
 
     a0, b0 = collapse(p_tiles, p_cols)
     halo = [(lax.ppermute(a0, both, pairs_a), lax.ppermute(b0, both, pairs_b))]
     a1, b1, local, rh = first_half(a_tiles, a_cols, a_count, p_tiles, p_cols, a0, b0)
     halo.append((lax.ppermute(a1, both, pairs_a), lax.ppermute(b1, both, pairs_b)))
     local, rh = second_half(a_tiles, a_cols, a_count, a0, b0, a1, b1, local, rh)
-    tiles, edges = [], []
-    for group, (ha, hb) in zip(GROUPS, halo, strict=True):
-        done, edge = finish(group, ha, hb, rh, local, *edges)
-        tiles.append(done)
-        edges = [edge]
-    parts = list(split(tiles, lax.ppermute(edges[0], both, hop)))
-    for d in range(1, SUBS):
-        route = [(i, i ^ d) for i in range(SUBS)]
-        parts[d] = lax.ppermute(parts[d], "sub", route)
-    return gather_parts(parts)
+    done = [finish(group, ha, hb, rh, local) for group, (ha, hb) in zip(GROUPS, halo, strict=True)]
+    tiles = [t for t, _ in done]
+    edges = [lax.ppermute(edge, both, hop) for _, edge in done]
+    kinds, parts = [], []
+    for groups, which in PLAN:
+        for d, part in zip(which, split(groups, which, tiles, edges), strict=True):
+            if d:
+                part = lax.ppermute(part, "sub", [(i, i ^ d) for i in range(SUBS)])
+            kinds.append((d, groups))
+            parts.append(part)
+    return gather_parts(kinds, parts)
 
 
 def solution(mesh):

time: 65.9 us -> 61.4 us (0.932); the launches traced: 64.8 us -> 61 us
  waiting for transfers between devices: 22.6 us -> 8.21 us
  starting transfers between devices: 14.7 us -> 25.3 us
    ppermute x4 -> x7, starting transfers between devices: 9.03 us -> 19.6 us  [the longest x2 11.3 us: shards(): edges = [lax.ppermute(edge, both, hop) for _, edge in done]]
    ppermute x1, waiting for transfers between devices: 8.97 us -> 1.1 us  [shards(): lax.ppermute(a1, both, pairs_a)]
    ppermute x4 -> x7, waiting for transfers between devices: 13.2 us -> 6.71 us  [the longest x5 5.11 us: shards(): part = lax.ppermute(part, 'sub', [(i, i ^ d) for i in range(SUBS)])]
    pallas_call x2 -> x4, Pallas kernels: 1.36 us -> 1.39 us  [the longest x1 1.23 us: gather_parts(): pl.pallas_call(kernel, out_shape=jax.ShapeDtypeStruct((8, 7, WIDE, TILE),...]
  transfers between devices with their start and end apart: 8 -> 11, of which waited for: 5 -> 5; matrix products, arithmetic and copies ran while one was open for 0% -> 0% of each run, Pallas kernels for 33% -> 36%
where the time goes in v3:
time: 61.4 us; the launch traced here: 61 us
  Pallas kernels  26.6 us (43%)
  starting transfers between devices  25.3 us (41%)
  waiting for transfers between devices  8.21 us (13%)
  local copies, waits for them, and re-layouts  0.85 us (1%)
    ppermute x2, starting transfers between devices, shards(): edges = [lax.ppermute(edge, both, hop) for _, edge in done]  11.3 us
    pallas_call x1, Pallas kernels, first_half(): pl.pallas_call(first_kernel, out_shape=[shape, shape] + LOCAL, in_specs=[...  10.6 us
    pallas_call x1, Pallas kernels, second_half(): pl.pallas_call(second_kernel, out_shape=LOCAL, in_specs=[SMEM, SMEM, HBM]...  9.39 us
    ppermute x5, starting transfers between devices, shards(): part = lax.ppermute(part, 'sub', [(i, i ^ d) for i in range(SUBS)])  8.32 us
    ppermute x5, waiting for transfers between devices, shards(): part = lax.ppermute(part, 'sub', [(i, i ^ d) for i in range(SUBS)])  5.11 us
    ppermute x2, starting transfers between devices, shards(): halo = [(lax.ppermute(a0, both, pairs_a), lax.ppermute(b0, both, pairs_b))]  3.26 us
    pallas_call x1, Pallas kernels, collapse(): pl.pallas_call(collapse_kernel, out_shape=[shape, shape], in_specs=[SMEM,...  3.11 us
    pallas_call x2, Pallas kernels, finish(): pl.pallas_call(kernel, out_shape=[jax.ShapeDtypeStruct((2, count, TILE, T...  2.1 us
  transfers between devices with their start and end apart: 11, of which 5 were waited for; matrix products, arithmetic and copies ran while one was open for 0% of the time, Pallas kernels for 36%

profile of v3, /device:TPU:38, one launch (start us, length us, event | category | flops | bytes accessed | tf_op | source)
XLA Modules:
  0.0 61.0 jit_solution(181419991943951623)
XLA Ops:
  0.0 0.8 %copy-done.1 = s32[32,4]{0,1:T(4,128)S(1)} copy-done((s32[32,4]{0,1:T(4,128)S(1)}, s32[32,4]{0,1:T(4,128)}, u32[]{:S(2)}) %copy-start.1) | copy-done | bytes 536
  0.8 3.1 %shard_map.55 = (bf16[2,16,128,128]{3,2,1,0:T(8,128)(2,1)S(1)}, bf16[2,16,128,128]{3,2,1,0:T(8,128)(2,1)S(1)}) custom-call(s32[4,32]{1,0:T(4,128)S(1)} %bitcast.2, bf16[32,4,128,128]{3,2,1,0:T(8,128)(2,1)} %p_hbm.3), custom_call_target="tpu_custom_call" | custom-call | flops 8388608 | bytes 6291456 | tf_op jit(solution)/shard_map/pallas_call | solution.py:89
  4.0 1.7 %collective-permute-start = (bf16[2,16,128,128]{3,2,1,0:T(8,128)(2,1)S(1)}, bf16[2,16,128,128]{3,2,1,0:T(8,128)(2,1)S(1)}, u32[]{:S(2)}, u32[]{:S(2)}) collective-permute-start(bf16[2,16,128,128]{3,2,1,0:T(8,128)(2,1)S(1)} %get-tuple-element.23.a0), channel_id=1, source_target_pairs={{0,1},{1,0},{2,3},{3,2},{4,5},{5,4},{6,7},{7,6},{8,9},{9,8},{10,11... | collective-permute-start | bytes 3145736 | tf_op jit(solution)/shard_map/ppermute | solution.py:406
  5.6 1.6 %collective-permute-start.1 = (bf16[2,16,128,128]{3,2,1,0:T(8,128)(2,1)S(1)}, bf16[2,16,128,128]{3,2,1,0:T(8,128)(2,1)S(1)}, u32[]{:S(2)}, u32[]{:S(2)}) collective-permute-start(bf16[2,16,128,128]{3,2,1,0:T(8,128)(2,1)S(1)} %get-tuple-element.24.b0), channel_id=1, source_target_pairs={{0,127},{1,2},{2,1},{3,4},{4,3},{5,6},{6,5},{7,8},{8,7},{9,10},{10... | collective-permute-start | bytes 3145736 | tf_op jit(solution)/shard_map/ppermute | solution.py:406
  7.2 10.6 %shard_map.56 = (bf16[1,16,128,128]{3,2,1,0:T(8,128)(2,1)S(1)}, bf16[1,16,128,128]{3,2,1,0:T(8,128)(2,1)S(1)}, f32[2,5,384,128]{3,2,1,0:T(8,128)S(1)}, bf16[2,384,2048]{2,1,0:T(8,128)(2,1)S(1)}) custom-call(s32[8,32]{1,0:T(8,128)S(1)} %bitcast.4, s32[32]{0:T(128)S(1)} %copy-done.4, s32[4,32]{1,0:T(4,128)S(1)} %bitcast.3, bf16[32,8,128,128]{3,2,1,0:T(8,128)(2,1)} %a_hbm.3, ...), custom_call_target="tpu_custom_call" | custom-call | flops 8589934592 | bytes 8388608 | tf_op jit(solution)/shard_map/pallas_call | solution.py:200
  17.9 1.3 %collective-permute-start.5 = (bf16[1,16,128,128]{3,2,1,0:T(8,128)(2,1)S(1)}, bf16[1,16,128,128]{3,2,1,0:T(8,128)(2,1)S(1)}, u32[]{:S(2)}, u32[]{:S(2)}) collective-permute-start(bf16[1,16,128,128]{3,2,1,0:T(8,128)(2,1)S(1)} %get-tuple-element.25.a1), channel_id=1, source_target_pairs={{0,1},{1,0},{2,3},{3,2},{4,5},{5,4},{6,7},{7,6},{8,9},{9,8},{10,11... | collective-permute-start | bytes 1572872 | tf_op jit(solution)/shard_map/ppermute | solution.py:408
  19.2 1.1 %collective-permute-start.6 = (bf16[1,16,128,128]{3,2,1,0:T(8,128)(2,1)S(1)}, bf16[1,16,128,128]{3,2,1,0:T(8,128)(2,1)S(1)}, u32[]{:S(2)}, u32[]{:S(2)}) collective-permute-start(bf16[1,16,128,128]{3,2,1,0:T(8,128)(2,1)S(1)} %get-tuple-element.26.b1), channel_id=1, source_target_pairs={{0,127},{1,2},{2,1},{3,4},{4,3},{5,6},{6,5},{7,8},{8,7},{9,10},{10... | collective-permute-start | bytes 1572872 | tf_op jit(solution)/shard_map/ppermute | solution.py:408
  20.3 9.4 %shard_map.57 = (f32[2,5,384,128]{3,2,1,0:T(8,128)S(1)}, bf16[2,384,2048]{2,1,0:T(8,128)(2,1)S(1)}) custom-call(s32[8,32]{1,0:T(8,128)S(1)} %bitcast.5, s32[32]{0:T(128)S(1)} %copy-done.4, bf16[32,8,128,128]{3,2,1,0:T(8,128)(2,1)} %a_hbm.3, bf16[2,16,128,128]{3,2,1,0:T(8,128)(2,1)S(1)} %get-tuple-element.23.a0, ...), custom_call_target="tpu_custom_call", output_to_operand_aliasing={{0}: (7, {}), {1}: (8, {})} | custom-call | flops 8589934592 | bytes 8388608 | tf_op jit(solution)/shard_map/pallas_call | solution.py:219
  29.7 0.4 collective-permute-done.refs_0_
  30.1 1.1 %shard_map.58 = (f32[2,8,128,128]{3,2,1,0:T(8,128)S(1)}, bf16[4,128,128]{2,1,0:T(8,128)(2,1)S(1)}) custom-call(bf16[2,16,128,128]{3,2,1,0:T(8,128)(2,1)S(1)} %collective-permute-done.refs_0_, bf16[2,16,128,128]{3,2,1,0:T(8,128)(2,1)S(1)} %collective-permute-done.1.refs_1_, bf16[2,384,2048]{2,1,0:T(8,128)(2,1)S(1)} %get-tuple-element.29.refs_2_, ...), custom_call_target="tpu_custom_call" | custom-call | flops 419430400 | bytes 6291456 | tf_op jit(solution)/shard_map/pallas_call | solution.py:298
  31.2 7.9 %collective-permute-start.2 = (bf16[4,128,128]{2,1,0:T(8,128)(2,1)S(1)}, bf16[4,128,128]{2,1,0:T(8,128)(2,1)S(1)}, u32[]{:S(2)}, u32[]{:S(2)}) collective-permute-start(bf16[4,128,128]{2,1,0:T(8,128)(2,1)S(1)} %get-tuple-element.32), channel_id=1, source_target_pairs={{124,120},{120,116},{116,112},{112,108},{108,104},{104,100},{100,9... | collective-permute-start | bytes 393224 | tf_op jit(solution)/shard_map/ppermute | solution.py:412
  39.1 1.1 %collective-permute-done.5.refs_0_ = bf16[1,16,128,128]{3,2,1,0:T(8,128)(2,1)S(1)} collective-permute-done((bf16[1,16,128,128]{3,2,1,0:T(8,128)(2,1)S(1)}, bf16[1,16,128,128]{3,2,1,0:T(8,128)(2,1)S(1)}, u32[]{:S(2)}, u32[]{:S(2)}) %collective-permute-start.5) | collective-permute-done | bytes 524320 | tf_op jit(solution)/shard_map/ppermute | solution.py:408
  40.2 0.0 collective-permute-done.6.refs_1_
  40.2 1.0 %shard_map.60 = (f32[2,3,128,128]{3,2,1,0:T(8,128)S(1)}, bf16[1,128,128]{2,1,0:T(8,128)(2,1)S(1)}) custom-call(bf16[1,16,128,128]{3,2,1,0:T(8,128)(2,1)S(1)} %collective-permute-done.5.refs_0_, bf16[1,16,128,128]{3,2,1,0:T(8,128)(2,1)S(1)} %collective-permute-done.6.refs_1_, bf16[2,384,2048]{2,1,0:T(8,128)(2,1)S(1)} %get-tuple-element.29.refs_2_, ...), custom_call_target="tpu_custom_call" | custom-call | flops 419430400 | bytes 6291456 | tf_op jit(solution)/shard_map/pallas_call | solution.py:298
  41.2 3.4 %collective-permute-start.7 = (bf16[1,128,128]{2,1,0:T(8,128)(2,1)S(1)}, bf16[1,128,128]{2,1,0:T(8,128)(2,1)S(1)}, u32[]{:S(2)}, u32[]{:S(2)}) collective-permute-start(bf16[1,128,128]{2,1,0:T(8,128)(2,1)S(1)} %get-tuple-element.37), channel_id=1, source_target_pairs={{124,120},{120,116},{116,112},{112,108},{108,104},{104,100},{100,9... | collective-permute-start | bytes 98312 | tf_op jit(solution)/shard_map/ppermute | solution.py:412
  44.6 1.6 %collective-permute-done.7.refs_1_.refs_3_ = bf16[1,128,128]{2,1,0:T(8,128)(2,1)S(1)} collective-permute-done((bf16[1,128,128]{2,1,0:T(8,128)(2,1)S(1)}, bf16[1,128,128]{2,1,0:T(8,128)(2,1)S(1)}, u32[]{:S(2)}, u32[]{:S(2)}) %collective-permute-start.7) | collective-permute-done | bytes 32800 | tf_op jit(solution)/shard_map/ppermute | solution.py:412
  46.2 0.9 %collective-permute-start.10 = (bf16[2,11,32,128]{3,2,1,0:T(8,128)(2,1)S(1)}, bf16[2,11,32,128]{3,2,1,0:T(8,128)(2,1)S(1)}, u32[]{:S(2)}, u32[]{:S(2)}) collective-permute-start(bf16[2,11,32,128]{3,2,1,0:T(8,128)(2,1)S(1)} %shard_map.62), channel_id=1, source_target_pairs={{0,2},{1,3},{2,0},{3,1},{4,6},{5,7},{6,4},{7,5},{8,10},{9,11},{10,... | collective-permute-start | bytes 540680 | tf_op jit(solution)/shard_map/ppermute | solution.py:417
  47.2 0.1 shard_map.59
  47.2 4.0 %collective-permute-start.3 = (bf16[2,8,32,128]{3,2,1,0:T(8,128)(2,1)S(1)}, bf16[2,8,32,128]{3,2,1,0:T(8,128)(2,1)S(1)}, u32[]{:S(2)}, u32[]{:S(2)}) collective-permute-start(bf16[2,8,32,128]{3,2,1,0:T(8,128)(2,1)S(1)} %get-tuple-element.34), channel_id=1, source_target_pairs={{0,1},{1,0},{2,3},{3,2},{4,5},{5,4},{6,7},{7,6},{8,9},{9,8},{10,11... | collective-permute-start | bytes 393224 | tf_op jit(solution)/shard_map/ppermute | solution.py:417
  51.3 0.7 %collective-permute-start.8 = (bf16[2,3,32,128]{3,2,1,0:T(8,128)(2,1)S(1)}, bf16[2,3,32,128]{3,2,1,0:T(8,128)(2,1)S(1)}, u32[]{:S(2)}, u32[]{:S(2)}) collective-permute-start(bf16[2,3,32,128]{3,2,1,0:T(8,128)(2,1)S(1)} %get-tuple-element.39), channel_id=1, source_target_pairs={{0,1},{1,0},{2,3},{3,2},{4,5},{5,4},{6,7},{7,6},{8,9},{9,8},{10,11... | collective-permute-start | bytes 147464 | tf_op jit(solution)/shard_map/ppermute | solution.py:417
  52.0 2.7 %collective-permute-start.9 = (bf16[2,3,32,128]{3,2,1,0:T(8,128)(2,1)S(1)}, bf16[2,3,32,128]{3,2,1,0:T(8,128)(2,1)S(1)}, u32[]{:S(2)}, u32[]{:S(2)}) collective-permute-start(bf16[2,3,32,128]{3,2,1,0:T(8,128)(2,1)S(1)} %get-tuple-element.40), channel_id=1, source_target_pairs={{0,3},{1,2},{2,1},{3,0},{4,7},{5,6},{6,5},{7,4},{8,11},{9,10},{10,... | collective-permute-start | bytes 147464 | tf_op jit(solution)/shard_map/ppermute | solution.py:417
  54.7 4.3 %collective-permute-done.8.refs_4_ = bf16[2,3,32,128]{3,2,1,0:T(8,128)(2,1)S(1)} collective-permute-done((bf16[2,3,32,128]{3,2,1,0:T(8,128)(2,1)S(1)}, bf16[2,3,32,128]{3,2,1,0:T(8,128)(2,1)S(1)}, u32[]{:S(2)}, u32[]{:S(2)}) %collective-permute-start.8) | collective-permute-done | bytes 49184 | tf_op jit(solution)/shard_map/ppermute | solution.py:417
  59.0 0.8 %collective-permute-done.9.refs_5_ = bf16[2,3,32,128]{3,2,1,0:T(8,128)(2,1)S(1)} collective-permute-done((bf16[2,3,32,128]{3,2,1,0:T(8,128)(2,1)S(1)}, bf16[2,3,32,128]{3,2,1,0:T(8,128)(2,1)S(1)}, u32[]{:S(2)}, u32[]{:S(2)}) %collective-permute-start.9) | collective-permute-done | bytes 49184 | tf_op jit(solution)/shard_map/ppermute | solution.py:417
  59.8 1.2 %shard_map.63 = f32[8,7,32,128]{3,2,1,0:T(8,128)} custom-call(bf16[2,8,32,128]{3,2,1,0:T(8,128)(2,1)S(1)} %get-tuple-element.33.refs_0_, bf16[2,8,32,128]{3,2,1,0:T(8,128)(2,1)S(1)} %collective-permute-done.3.refs_1_, bf16[2,8,32,128]{3,2,1,0:T(8,128)(2,1)S(1)} %collective-permute-done.4.refs_2_, bf16[2,3,32,128]{3,2,1,0:T(8,128)(2,1)S(1)} %get-tuple-element.38.refs_3_, ...), custom_call_target="tpu_custom_call" | custom-call | tf_op jit(solution)/shard_map/pallas_call | solution.py:382
  (17 shorter events, 0.1 us)
Async XLA Ops:
  0.0 7.2 %copy-start = (bf16[32,4,128,128]{3,2,1,0:T(8,128)(2,1)S(1)}, bf16[32,4,128,128]{3,2,1,0:T(8,128)(2,1)}, u32[]{:S(2)}) copy-start(bf16[32,4,128,128]{3,2,1,0:T(8,128)(2,1)} %p_hbm.3) | copy-start | bytes 12582916
  0.0 0.8 %copy-start.1 = (s32[32,4]{0,1:T(4,128)S(1)}, s32[32,4]{0,1:T(4,128)}, u32[]{:S(2)}) copy-start(s32[32,4]{0,1:T(4,128)} %param.9) | copy-start | bytes 1540
  0.8 6.4 %copy-start.2 = (s32[32,4]{0,1:T(4,128)S(1)}, s32[32,4]{0,1:T(4,128)}, u32[]{:S(2)}) copy-start(s32[32,4]{0,1:T(4,128)} %param.9) | copy-start | bytes 1540
  0.8 6.4 %copy-start.3 = (s32[32,8]{0,1:T(8,128)S(1)}, s32[32,8]{0,1:T(8,128)}, u32[]{:S(2)}) copy-start(s32[32,8]{0,1:T(8,128)} %param.6) | copy-start | bytes 3076
  0.8 6.4 %copy-start.4 = (s32[32]{0:T(128)S(1)}, s32[32]{0:T(128)}, u32[]{:S(2)}) copy-start(s32[32]{0:T(128)} %acount.3) | copy-start | bytes 388
  4.0 26.1 %collective-permute-start = (bf16[2,16,128,128]{3,2,1,0:T(8,128)(2,1)S(1)}, bf16[2,16,128,128]{3,2,1,0:T(8,128)(2,1)S(1)}, u32[]{:S(2)}, u32[]{:S(2)}) collective-permute-start(bf16[2,16,128,128]{3,2,1,0:T(8,128)(2,1)S(1)} %get-tuple-element.23.a0), channel_id=1, source_target_pairs={{0,1},{1,0},{2,3},{3,2},{4,5},{5,4},{6,7},{7,6},{8,9},{9,8},{10,11... | collective-permute-start | bytes 3145736 | tf_op jit(solution)/shard_map/ppermute | solution.py:406
  5.6 24.5 %collective-permute-start.1 = (bf16[2,16,128,128]{3,2,1,0:T(8,128)(2,1)S(1)}, bf16[2,16,128,128]{3,2,1,0:T(8,128)(2,1)S(1)}, u32[]{:S(2)}, u32[]{:S(2)}) collective-permute-start(bf16[2,16,128,128]{3,2,1,0:T(8,128)(2,1)S(1)} %get-tuple-element.24.b0), channel_id=1, source_target_pairs={{0,127},{1,2},{2,1},{3,4},{4,3},{5,6},{6,5},{7,8},{8,7},{9,10},{10... | collective-permute-start | bytes 3145736 | tf_op jit(solution)/shard_map/ppermute | solution.py:406
  17.9 22.3 %collective-permute-start.5 = (bf16[1,16,128,128]{3,2,1,0:T(8,128)(2,1)S(1)}, bf16[1,16,128,128]{3,2,1,0:T(8,128)(2,1)S(1)}, u32[]{:S(2)}, u32[]{:S(2)}) collective-permute-start(bf16[1,16,128,128]{3,2,1,0:T(8,128)(2,1)S(1)} %get-tuple-element.25.a1), channel_id=1, source_target_pairs={{0,1},{1,0},{2,3},{3,2},{4,5},{5,4},{6,7},{7,6},{8,9},{9,8},{10,11... | collective-permute-start | bytes 1572872 | tf_op jit(solution)/shard_map/ppermute | solution.py:408
  19.2 21.0 %collective-permute-start.6 = (bf16[1,16,128,128]{3,2,1,0:T(8,128)(2,1)S(1)}, bf16[1,16,128,128]{3,2,1,0:T(8,128)(2,1)S(1)}, u32[]{:S(2)}, u32[]{:S(2)}) collective-permute-start(bf16[1,16,128,128]{3,2,1,0:T(8,128)(2,1)S(1)} %get-tuple-element.26.b1), channel_id=1, source_target_pairs={{0,127},{1,2},{2,1},{3,4},{4,3},{5,6},{6,5},{7,8},{8,7},{9,10},{10... | collective-permute-start | bytes 1572872 | tf_op jit(solution)/shard_map/ppermute | solution.py:408
  31.2 15.0 %collective-permute-start.2 = (bf16[4,128,128]{2,1,0:T(8,128)(2,1)S(1)}, bf16[4,128,128]{2,1,0:T(8,128)(2,1)S(1)}, u32[]{:S(2)}, u32[]{:S(2)}) collective-permute-start(bf16[4,128,128]{2,1,0:T(8,128)(2,1)S(1)} %get-tuple-element.32), channel_id=1, source_target_pairs={{124,120},{120,116},{116,112},{112,108},{108,104},{104,100},{100,9... | collective-permute-start | bytes 393224 | tf_op jit(solution)/shard_map/ppermute | solution.py:412
  41.2 5.0 %collective-permute-start.7 = (bf16[1,128,128]{2,1,0:T(8,128)(2,1)S(1)}, bf16[1,128,128]{2,1,0:T(8,128)(2,1)S(1)}, u32[]{:S(2)}, u32[]{:S(2)}) collective-permute-start(bf16[1,128,128]{2,1,0:T(8,128)(2,1)S(1)} %get-tuple-element.37), channel_id=1, source_target_pairs={{124,120},{120,116},{116,112},{112,108},{108,104},{104,100},{100,9... | collective-permute-start | bytes 98312 | tf_op jit(solution)/shard_map/ppermute | solution.py:412
  46.2 13.6 %collective-permute-start.10 = (bf16[2,11,32,128]{3,2,1,0:T(8,128)(2,1)S(1)}, bf16[2,11,32,128]{3,2,1,0:T(8,128)(2,1)S(1)}, u32[]{:S(2)}, u32[]{:S(2)}) collective-permute-start(bf16[2,11,32,128]{3,2,1,0:T(8,128)(2,1)S(1)} %shard_map.62), channel_id=1, source_target_pairs={{0,2},{1,3},{2,0},{3,1},{4,6},{5,7},{6,4},{7,5},{8,10},{9,11},{10,... | collective-permute-start | bytes 540680 | tf_op jit(solution)/shard_map/ppermute | solution.py:417
  47.2 12.5 %collective-permute-start.3 = (bf16[2,8,32,128]{3,2,1,0:T(8,128)(2,1)S(1)}, bf16[2,8,32,128]{3,2,1,0:T(8,128)(2,1)S(1)}, u32[]{:S(2)}, u32[]{:S(2)}) collective-permute-start(bf16[2,8,32,128]{3,2,1,0:T(8,128)(2,1)S(1)} %get-tuple-element.34), channel_id=1, source_target_pairs={{0,1},{1,0},{2,3},{3,2},{4,5},{5,4},{6,7},{7,6},{8,9},{9,8},{10,11... | collective-permute-start | bytes 393224 | tf_op jit(solution)/shard_map/ppermute | solution.py:417
  51.2 8.6 %collective-permute-start.4 = (bf16[2,8,32,128]{3,2,1,0:T(8,128)(2,1)S(1)}, bf16[2,8,32,128]{3,2,1,0:T(8,128)(2,1)S(1)}, u32[]{:S(2)}, u32[]{:S(2)}) collective-permute-start(bf16[2,8,32,128]{3,2,1,0:T(8,128)(2,1)S(1)} %get-tuple-element.35), channel_id=1, source_target_pairs={{0,3},{1,2},{2,1},{3,0},{4,7},{5,6},{6,5},{7,4},{8,11},{9,10},{10,... | collective-permute-start | bytes 393224 | tf_op jit(solution)/shard_map/ppermute | solution.py:417
  51.3 7.7 %collective-permute-start.8 = (bf16[2,3,32,128]{3,2,1,0:T(8,128)(2,1)S(1)}, bf16[2,3,32,128]{3,2,1,0:T(8,128)(2,1)S(1)}, u32[]{:S(2)}, u32[]{:S(2)}) collective-permute-start(bf16[2,3,32,128]{3,2,1,0:T(8,128)(2,1)S(1)} %get-tuple-element.39), channel_id=1, source_target_pairs={{0,1},{1,0},{2,3},{3,2},{4,5},{5,4},{6,7},{7,6},{8,9},{9,8},{10,11... | collective-permute-start | bytes 147464 | tf_op jit(solution)/shard_map/ppermute | solution.py:417
  52.0 7.8 %collective-permute-start.9 = (bf16[2,3,32,128]{3,2,1,0:T(8,128)(2,1)S(1)}, bf16[2,3,32,128]{3,2,1,0:T(8,128)(2,1)S(1)}, u32[]{:S(2)}, u32[]{:S(2)}) collective-permute-start(bf16[2,3,32,128]{3,2,1,0:T(8,128)(2,1)S(1)} %get-tuple-element.40), channel_id=1, source_target_pairs={{0,3},{1,2},{2,1},{3,0},{4,7},{5,6},{6,5},{7,4},{8,11},{9,10},{10,... | collective-permute-start | bytes 147464 | tf_op jit(solution)/shard_map/ppermute | solution.py:417

commit v4 on v3

--- a/solution.py
+++ b/solution.py
@@ -17,7 +17,7 @@
 MIB = 1 << 20
 STEP = 4
 GROUPS = ((0, 1), (2,))
-PLAN = (((0,), (0, 1, 3)), ((1,), (0, 1, 3)), ((0, 1), (2,)))
+PLAN = (((0, 1), (2,)), ((0, 1), (0, 1, 3)))
 VMEM = pl.BlockSpec(memory_space=pltpu.VMEM)
 SMEM = pl.BlockSpec(memory_space=pltpu.SMEM)
 HBM = pl.BlockSpec(memory_space=pltpu.HBM)
@@ -251,7 +251,7 @@
     return sorted(below, key=lambda b: b[2]), sorted(above, key=lambda b: b[2])
 
 
-def finish_kernel(group, ha_ref, hb_ref, rh_ref, out_ref, tiles, edge):
+def finish_kernel(group, ha_ref, hb_ref, rh_ref, out_ref, tiles, *edge):
     device, sub, parity = place()
     for x, halo in enumerate((ha_ref, hb_ref)):
         side = x ^ (1 - parity)
@@ -275,39 +275,71 @@
                 for t in range(3):
                     tiles[side, first + t] = part[t * TILE : (t + 1) * TILE]
             first += len(tiles_of(chunk))
+    if not edge:
+        return
     below, above = edge_tiles(group)
 
     @pl.when(sub == 0)
     def _():
         for n, (side, at, _j) in enumerate(below):
-            edge[n] = tiles[side, at].astype(BF16)
+            edge[0][n] = tiles[side, at].astype(BF16)
 
     @pl.when(sub == SUBS - 1)
     def _():
         for n, (side, at, _j) in enumerate(above):
-            edge[n] = tiles[side, at].astype(BF16)
-
-
-def finish(group, ha, hb, rh, local):
+            edge[0][n] = tiles[side, at].astype(BF16)
+
+
+def last_edge_kernel(hb_ref, rh_ref, out_ref, edge):
+    device, sub, parity = place()
+
+    def one(side, t):
+        rows = slice(t * TILE, (t + 1) * TILE)
+        part = jnp.dot(
+            rh_ref[side, rows, :], hb_ref[0].reshape(AGG * TILE, TILE), preferred_element_type=F32
+        )
+        edge[0] = (part + out_ref[side, 4 * side, rows]).astype(BF16)
+
+    @pl.when(sub < SUBS - 1)
+    def _():
+        one(0, 0)
+
+    @pl.when(sub == SUBS - 1)
+    def _():
+        one(1, 2)
+
+
+def last_edge(hb, rh, local):
+    return pl.pallas_call(
+        last_edge_kernel,
+        out_shape=jax.ShapeDtypeStruct((1, TILE, TILE), BF16),
+        in_specs=[VMEM] * 3,
+        out_specs=VMEM,
+        compiler_params=pltpu.CompilerParams(vmem_limit_bytes=24 * MIB),
+        cost_estimate=pl.CostEstimate(flops=64 * MIB, bytes_accessed=MIB, transcendentals=0),
+    )(hb, rh, local)
+
+
+def finish(group, with_edge, ha, hb, rh, local, *after):
     count = sum(len(tiles_of(c)) for c in group)
-    edges = len(edge_tiles(group)[0])
+    shapes = [jax.ShapeDtypeStruct((2, count, TILE, TILE), F32)]
+    if with_edge:
+        edges = len(edge_tiles(group)[0])
+        shapes.append(jax.ShapeDtypeStruct((edges, TILE, TILE), BF16))
 
     def kernel(*refs):
-        finish_kernel(group, *refs)
+        finish_kernel(group, *refs[:4], *refs[4 + len(after) :])
 
     return pl.pallas_call(
         kernel,
-        out_shape=[
-            jax.ShapeDtypeStruct((2, count, TILE, TILE), F32),
-            jax.ShapeDtypeStruct((edges, TILE, TILE), BF16),
-        ],
-        in_specs=[VMEM] * 4,
-        out_specs=[VMEM] * 2,
+        out_shape=shapes,
+        in_specs=[VMEM] * (4 + len(after)),
+        out_specs=[VMEM] * len(shapes),
         compiler_params=pltpu.CompilerParams(vmem_limit_bytes=24 * MIB),
         cost_estimate=pl.CostEstimate(
             flops=400 * MIB, bytes_accessed=6 * MIB, transcendentals=0
         ),
-    )(ha, hb, rh, local)
+    )(ha, hb, rh, local, *after)
 
 
 def split_kernel(groups, which, *refs):
@@ -338,27 +370,27 @@
             base += tiles.shape[1]
 
 
-def split(groups, which, tiles, edges):
+def split(groups, which, tiles, edges, *after):
     count = sum(tiles[g].shape[1] for g in groups)
     shape = jax.ShapeDtypeStruct((2, count, WIDE, TILE), BF16)
 
     def kernel(*refs):
-        split_kernel(groups, which, *refs)
+        split_kernel(groups, which, *refs[: 2 * len(groups)], *refs[2 * len(groups) + len(after) :])
 
     return pl.pallas_call(
         kernel,
         out_shape=[shape] * len(which),
-        in_specs=[VMEM] * (2 * len(groups)),
+        in_specs=[VMEM] * (2 * len(groups) + len(after)),
         out_specs=[VMEM] * len(which),
         compiler_params=pltpu.CompilerParams(vmem_limit_bytes=16 * MIB),
-    )(*[x for g in groups for x in (tiles[g], edges[g])])
+    )(*[x for g in groups for x in (tiles[g], edges[g])], *after)
 
 
 def gather_kernel(kinds, *refs):
     parts = refs[: len(kinds)]
-    out_ref, window = refs[len(kinds) :]
-    device, sub, parity = place()
-    window[...] = jnp.zeros_like(window)
+    out_ref = refs[len(kinds)]
+    device, sub, parity = place()
+    out_ref[...] = jnp.zeros_like(out_ref)
     for (d, groups), part in zip(kinds, parts, strict=True):
         first = 2 * (sub ^ d)
         at = 0
@@ -370,9 +402,8 @@
                     if 0 <= column - i + 4 < 7:
                         row = first + i - 1
                         row = jnp.where(row < 0, 7, jnp.where(row > 7, 0, row))
-                        window[row, column - i + 4] += part[side, at].astype(F32)
+                        out_ref[row, column - i + 4] += part[side, at].astype(F32)
                 at += 1
-    out_ref[...] = window[...]
 
 
 def gather_parts(kinds, parts):
@@ -384,7 +415,6 @@
         out_shape=jax.ShapeDtypeStruct((8, 7, WIDE, TILE), F32),
         in_specs=[VMEM] * len(parts),
         out_specs=VMEM,
-        scratch_shapes=[pltpu.VMEM((8, 7, WIDE, TILE), F32)],
         compiler_params=pltpu.CompilerParams(vmem_limit_bytes=16 * MIB),
     )(*parts)
 
@@ -407,12 +437,16 @@
     a1, b1, local, rh = first_half(a_tiles, a_cols, a_count, p_tiles, p_cols, a0, b0)
     halo.append((lax.ppermute(a1, both, pairs_a), lax.ppermute(b1, both, pairs_b)))
     local, rh = second_half(a_tiles, a_cols, a_count, a0, b0, a1, b1, local, rh)
-    done = [finish(group, ha, hb, rh, local) for group, (ha, hb) in zip(GROUPS, halo, strict=True)]
-    tiles = [t for t, _ in done]
-    edges = [lax.ppermute(edge, both, hop) for _, edge in done]
-    kinds, parts = [], []
+    tiles0, edge0 = finish(GROUPS[0], True, *halo[0], rh, local)
+    edge1 = last_edge(halo[1][1], rh, local)
+    (tiles1,) = finish(GROUPS[1], False, *halo[1], rh, local, edge1)
+    tiles = [tiles0, tiles1]
+    edges = [lax.ppermute(edge, both, hop) for edge in (edge0, edge1)]
+    kinds, parts, first = [], [], []
     for groups, which in PLAN:
-        for d, part in zip(which, split(groups, which, tiles, edges), strict=True):
+        cut = split(groups, which, tiles, edges, *first)
+        first = cut if len(which) == 1 else []
+        for d, part in zip(which, cut, strict=True):
             if d:
                 part = lax.ppermute(part, "sub", [(i, i ^ d) for i in range(SUBS)])
             kinds.append((d, groups))

time: 61.4 us -> 60.3 us (0.982)
  starting transfers between devices: 25.3 us -> 23.4 us
  waiting for transfers between devices: 8.21 us -> 9.03 us
    ppermute x5 -> x3, starting transfers between devices: 8.32 us -> 5.47 us  [shards(): part = lax.ppermute(part, 'sub', [(i, i ^ d) for i in range(SUBS)])]
    ppermute x5 -> x3, waiting for transfers between devices: 5.11 us -> 7.93 us  [shards(): part = lax.ppermute(part, 'sub', [(i, i ^ d) for i in range(SUBS)])]
    ppermute x1, starting transfers between devices: 1.34 us -> 0.01 us  [shards(): lax.ppermute(a1, both, pairs_a)]
    ppermute x1, starting transfers between devices: 1.09 us -> 2.33 us  [shards(): lax.ppermute(b1, both, pairs_b)]
    ppermute x2, starting transfers between devices: 11.3 us -> 12.4 us  [shards(): edges = [lax.ppermute(edge, both, hop) for edge in (edge0, edge1)]]
    ppermute x1, waiting for transfers between devices: 1.1 us -> 0.01 us  [shards(): lax.ppermute(a1, both, pairs_a)]
    ppermute x2, waiting for transfers between devices: 1.6 us -> 0.6 us  [shards(): edges = [lax.ppermute(edge, both, hop) for edge in (edge0, edge1)]]
    pallas_call x2 -> x3, Pallas kernels: 2.1 us -> 2.4 us  [the longest x2 2.1 us: finish(): pl.pallas_call(kernel, out_shape=shapes, in_specs=[VMEM] * (4 + len(after...]
  transfers between devices with their start and end apart: 11 -> 9, of which waited for: 5 -> 5; matrix products, arithmetic and copies ran while one was open for 0% -> 0% of each run, Pallas kernels for 36% -> 37%
where the time goes in v4:
time: 60.3 us; the launch traced here: 60.2 us
  Pallas kernels  26.8 us (44%)
  starting transfers between devices  23.4 us (39%)
  waiting for transfers between devices  9.03 us (15%)
  local copies, waits for them, and re-layouts  0.85 us (1%)
    ppermute x2, starting transfers between devices, shards(): edges = [lax.ppermute(edge, both, hop) for edge in (edge0, edge1)]  12.4 us
    pallas_call x1, Pallas kernels, first_half(): pl.pallas_call(first_kernel, out_shape=[shape, shape] + LOCAL, in_specs=[...  10.6 us
    pallas_call x1, Pallas kernels, second_half(): pl.pallas_call(second_kernel, out_shape=LOCAL, in_specs=[SMEM, SMEM, HBM]...  9.39 us
    ppermute x3, waiting for transfers between devices, shards(): part = lax.ppermute(part, 'sub', [(i, i ^ d) for i in range(SUBS)])  7.93 us
    ppermute x3, starting transfers between devices, shards(): part = lax.ppermute(part, 'sub', [(i, i ^ d) for i in range(SUBS)])  5.47 us
    ppermute x2, starting transfers between devices, shards(): halo = [(lax.ppermute(a0, both, pairs_a), lax.ppermute(b0, both, pairs_b))]  3.26 us
    pallas_call x1, Pallas kernels, collapse(): pl.pallas_call(collapse_kernel, out_shape=[shape, shape], in_specs=[SMEM,...  3.11 us
    ppermute x1, starting transfers between devices, shards(): lax.ppermute(b1, both, pairs_b)  2.33 us
  transfers between devices with their start and end apart: 9, of which 5 were waited for; matrix products, arithmetic and copies ran while one was open for 0% of the time, Pallas kernels for 37%

profile of v4, /device:TPU:38, one launch (start us, length us, event | category | flops | bytes accessed | tf_op | source)
XLA Modules:
  0.0 60.2 jit_solution(6261952991700672220)
XLA Ops:
  0.0 0.8 %copy-done.1 = s32[32,4]{0,1:T(4,128)S(1)} copy-done((s32[32,4]{0,1:T(4,128)S(1)}, s32[32,4]{0,1:T(4,128)}, u32[]{:S(2)}) %copy-start.1) | copy-done | bytes 536
  0.8 3.1 %shard_map.55 = (bf16[2,16,128,128]{3,2,1,0:T(8,128)(2,1)S(1)}, bf16[2,16,128,128]{3,2,1,0:T(8,128)(2,1)S(1)}) custom-call(s32[4,32]{1,0:T(4,128)S(1)} %bitcast.2, bf16[32,4,128,128]{3,2,1,0:T(8,128)(2,1)} %p_hbm.3), custom_call_target="tpu_custom_call" | custom-call | flops 8388608 | bytes 6291456 | tf_op jit(solution)/shard_map/pallas_call | solution.py:89
  4.0 1.7 %collective-permute-start = (bf16[2,16,128,128]{3,2,1,0:T(8,128)(2,1)S(1)}, bf16[2,16,128,128]{3,2,1,0:T(8,128)(2,1)S(1)}, u32[]{:S(2)}, u32[]{:S(2)}) collective-permute-start(bf16[2,16,128,128]{3,2,1,0:T(8,128)(2,1)S(1)} %get-tuple-element.18.a0), channel_id=1, source_target_pairs={{0,1},{1,0},{2,3},{3,2},{4,5},{5,4},{6,7},{7,6},{8,9},{9,8},{10,11... | collective-permute-start | bytes 3145736 | tf_op jit(solution)/shard_map/ppermute | solution.py:436
  5.6 1.6 %collective-permute-start.1 = (bf16[2,16,128,128]{3,2,1,0:T(8,128)(2,1)S(1)}, bf16[2,16,128,128]{3,2,1,0:T(8,128)(2,1)S(1)}, u32[]{:S(2)}, u32[]{:S(2)}) collective-permute-start(bf16[2,16,128,128]{3,2,1,0:T(8,128)(2,1)S(1)} %get-tuple-element.19.b0), channel_id=1, source_target_pairs={{0,127},{1,2},{2,1},{3,4},{4,3},{5,6},{6,5},{7,8},{8,7},{9,10},{10... | collective-permute-start | bytes 3145736 | tf_op jit(solution)/shard_map/ppermute | solution.py:436
  7.2 10.6 %shard_map.56 = (bf16[1,16,128,128]{3,2,1,0:T(8,128)(2,1)S(1)}, bf16[1,16,128,128]{3,2,1,0:T(8,128)(2,1)S(1)}, f32[2,5,384,128]{3,2,1,0:T(8,128)S(1)}, bf16[2,384,2048]{2,1,0:T(8,128)(2,1)S(1)}) custom-call(s32[8,32]{1,0:T(8,128)S(1)} %bitcast.4, s32[32]{0:T(128)S(1)} %copy-done.4, s32[4,32]{1,0:T(4,128)S(1)} %bitcast.3, bf16[32,8,128,128]{3,2,1,0:T(8,128)(2,1)} %a_hbm.3, ...), custom_call_target="tpu_custom_call" | custom-call | flops 8589934592 | bytes 8388608 | tf_op jit(solution)/shard_map/pallas_call | solution.py:200
  17.9 2.3 %collective-permute-start.4 = (bf16[1,16,128,128]{3,2,1,0:T(8,128)(2,1)S(1)}, bf16[1,16,128,128]{3,2,1,0:T(8,128)(2,1)S(1)}, u32[]{:S(2)}, u32[]{:S(2)}) collective-permute-start(bf16[1,16,128,128]{3,2,1,0:T(8,128)(2,1)S(1)} %get-tuple-element.21.b1), channel_id=1, source_target_pairs={{0,127},{1,2},{2,1},{3,4},{4,3},{5,6},{6,5},{7,8},{8,7},{9,10},{10... | collective-permute-start | bytes 1572872 | tf_op jit(solution)/shard_map/ppermute | solution.py:438
  20.2 0.0 collective-permute-start.3
  20.2 9.4 %shard_map.57 = (f32[2,5,384,128]{3,2,1,0:T(8,128)S(1)}, bf16[2,384,2048]{2,1,0:T(8,128)(2,1)S(1)}) custom-call(s32[8,32]{1,0:T(8,128)S(1)} %bitcast.5, s32[32]{0:T(128)S(1)} %copy-done.4, bf16[32,8,128,128]{3,2,1,0:T(8,128)(2,1)} %a_hbm.3, bf16[2,16,128,128]{3,2,1,0:T(8,128)(2,1)S(1)} %get-tuple-element.18.a0, ...), custom_call_target="tpu_custom_call", output_to_operand_aliasing={{0}: (7, {}), {1}: (8, {})} | custom-call | flops 8589934592 | bytes 8388608 | tf_op jit(solution)/shard_map/pallas_call | solution.py:219
  29.6 0.5 collective-permute-done.refs_0_
  30.1 1.1 %shard_map.58 = (f32[2,8,128,128]{3,2,1,0:T(8,128)S(1)}, bf16[4,128,128]{2,1,0:T(8,128)(2,1)S(1)}) custom-call(bf16[2,16,128,128]{3,2,1,0:T(8,128)(2,1)S(1)} %collective-permute-done.refs_0_, bf16[2,16,128,128]{3,2,1,0:T(8,128)(2,1)S(1)} %collective-permute-done.1.refs_1_, bf16[2,384,2048]{2,1,0:T(8,128)(2,1)S(1)} %get-tuple-element.24.refs_2_.rh_ref, ...), custom_call_target="tpu_custom_call" | custom-call | flops 419430400 | bytes 6291456 | tf_op jit(solution)/shard_map/pallas_call | solution.py:333
  31.2 7.9 %collective-permute-start.2 = (bf16[4,128,128]{2,1,0:T(8,128)(2,1)S(1)}, bf16[4,128,128]{2,1,0:T(8,128)(2,1)S(1)}, u32[]{:S(2)}, u32[]{:S(2)}) collective-permute-start(bf16[4,128,128]{2,1,0:T(8,128)(2,1)S(1)} %get-tuple-element.27), channel_id=1, source_target_pairs={{124,120},{120,116},{116,112},{112,108},{108,104},{104,100},{100,9... | collective-permute-start | bytes 393224 | tf_op jit(solution)/shard_map/ppermute | solution.py:444
  39.1 0.3 shard_map.59.refs_4_
  39.4 4.5 %collective-permute-start.5 = (bf16[1,128,128]{2,1,0:T(8,128)(2,1)S(1)}, bf16[1,128,128]{2,1,0:T(8,128)(2,1)S(1)}, u32[]{:S(2)}, u32[]{:S(2)}) collective-permute-start(bf16[1,128,128]{2,1,0:T(8,128)(2,1)S(1)} %shard_map.59.refs_4_), channel_id=1, source_target_pairs={{124,120},{120,116},{116,112},{112,108},{108,104},{104,100},{100,9... | collective-permute-start | bytes 98312 | tf_op jit(solution)/shard_map/ppermute | solution.py:444
  43.9 0.0 collective-permute-done.3.refs_0_
  43.9 1.0 %shard_map.60.refs_2_ = f32[2,3,128,128]{3,2,1,0:T(8,128)S(1)} custom-call(bf16[1,16,128,128]{3,2,1,0:T(8,128)(2,1)S(1)} %collective-permute-done.3.refs_0_, bf16[1,16,128,128]{3,2,1,0:T(8,128)(2,1)S(1)} %collective-permute-done.4.hb_ref.refs_1_, bf16[2,384,2048]{2,1,0:T(8,128)(2,1)S(1)} %get-tuple-element.24.refs_2_.rh_ref, ...), custom_call_target="tpu_custom_call" | custom-call | flops 419430400 | bytes 6291456 | tf_op jit(solution)/shard_map/pallas_call | solution.py:333
  44.9 0.6 collective-permute-done.5.refs_3_
  45.5 0.1 shard_map.62
  45.7 0.9 %collective-permute-start.7 = (bf16[2,11,32,128]{3,2,1,0:T(8,128)(2,1)S(1)}, bf16[2,11,32,128]{3,2,1,0:T(8,128)(2,1)S(1)}, u32[]{:S(2)}, u32[]{:S(2)}) collective-permute-start(bf16[2,11,32,128]{3,2,1,0:T(8,128)(2,1)S(1)} %get-tuple-element.29), channel_id=1, source_target_pairs={{0,1},{1,0},{2,3},{3,2},{4,5},{5,4},{6,7},{7,6},{8,9},{9,8},{10,11... | collective-permute-start | bytes 540680 | tf_op jit(solution)/shard_map/ppermute | solution.py:451
  46.5 3.2 %collective-permute-start.8 = (bf16[2,11,32,128]{3,2,1,0:T(8,128)(2,1)S(1)}, bf16[2,11,32,128]{3,2,1,0:T(8,128)(2,1)S(1)}, u32[]{:S(2)}, u32[]{:S(2)}) collective-permute-start(bf16[2,11,32,128]{3,2,1,0:T(8,128)(2,1)S(1)} %get-tuple-element.30), channel_id=1, source_target_pairs={{0,3},{1,2},{2,1},{3,0},{4,7},{5,6},{6,5},{7,4},{8,11},{9,10},{10,... | collective-permute-start | bytes 540680 | tf_op jit(solution)/shard_map/ppermute | solution.py:451
  49.8 1.4 %collective-permute-start.6 = (bf16[2,11,32,128]{3,2,1,0:T(8,128)(2,1)S(1)}, bf16[2,11,32,128]{3,2,1,0:T(8,128)(2,1)S(1)}, u32[]{:S(2)}, u32[]{:S(2)}) collective-permute-start(bf16[2,11,32,128]{3,2,1,0:T(8,128)(2,1)S(1)} %shard_map.61.refs_4_), channel_id=1, source_target_pairs={{0,2},{1,3},{2,0},{3,1},{4,6},{5,7},{6,4},{7,5},{8,10},{9,11},{10,... | collective-permute-start | bytes 540680 | tf_op jit(solution)/shard_map/ppermute | solution.py:451
  51.1 0.1 collective-permute-done.7.refs_2_
  51.2 6.2 %collective-permute-done.8.refs_3_ = bf16[2,11,32,128]{3,2,1,0:T(8,128)(2,1)S(1)} collective-permute-done((bf16[2,11,32,128]{3,2,1,0:T(8,128)(2,1)S(1)}, bf16[2,11,32,128]{3,2,1,0:T(8,128)(2,1)S(1)}, u32[]{:S(2)}, u32[]{:S(2)}) %collective-permute-start.8) | collective-permute-done | bytes 180256 | tf_op jit(solution)/shard_map/ppermute | solution.py:451
  57.4 1.7 %collective-permute-done.6.refs_0_ = bf16[2,11,32,128]{3,2,1,0:T(8,128)(2,1)S(1)} collective-permute-done((bf16[2,11,32,128]{3,2,1,0:T(8,128)(2,1)S(1)}, bf16[2,11,32,128]{3,2,1,0:T(8,128)(2,1)S(1)}, u32[]{:S(2)}, u32[]{:S(2)}) %collective-permute-start.6) | collective-permute-done | bytes 180256 | tf_op jit(solution)/shard_map/ppermute | solution.py:451
  59.1 1.2 %shard_map.63 = f32[8,7,32,128]{3,2,1,0:T(8,128)} custom-call(bf16[2,11,32,128]{3,2,1,0:T(8,128)(2,1)S(1)} %collective-permute-done.6.refs_0_, bf16[2,11,32,128]{3,2,1,0:T(8,128)(2,1)S(1)} %get-tuple-element.28.refs_1_, bf16[2,11,32,128]{3,2,1,0:T(8,128)(2,1)S(1)} %collective-permute-done.7.refs_2_, bf16[2,11,32,128]{3,2,1,0:T(8,128)(2,1)S(1)} %collective-permute-done.8.refs_3_), custom_call_target="tpu_custom_call" | custom-call | tf_op jit(solution)/shard_map/pallas_call | solution.py:413
  (13 shorter events, 0.1 us)
Async XLA Ops:
  0.0 7.2 %copy-start = (bf16[32,4,128,128]{3,2,1,0:T(8,128)(2,1)S(1)}, bf16[32,4,128,128]{3,2,1,0:T(8,128)(2,1)}, u32[]{:S(2)}) copy-start(bf16[32,4,128,128]{3,2,1,0:T(8,128)(2,1)} %p_hbm.3) | copy-start | bytes 12582916
  0.0 0.8 %copy-start.1 = (s32[32,4]{0,1:T(4,128)S(1)}, s32[32,4]{0,1:T(4,128)}, u32[]{:S(2)}) copy-start(s32[32,4]{0,1:T(4,128)} %param.9) | copy-start | bytes 1540
  0.8 6.4 %copy-start.2 = (s32[32,4]{0,1:T(4,128)S(1)}, s32[32,4]{0,1:T(4,128)}, u32[]{:S(2)}) copy-start(s32[32,4]{0,1:T(4,128)} %param.9) | copy-start | bytes 1540
  0.8 6.4 %copy-start.3 = (s32[32,8]{0,1:T(8,128)S(1)}, s32[32,8]{0,1:T(8,128)}, u32[]{:S(2)}) copy-start(s32[32,8]{0,1:T(8,128)} %param.6) | copy-start | bytes 3076
  0.8 6.4 %copy-start.4 = (s32[32]{0:T(128)S(1)}, s32[32]{0:T(128)}, u32[]{:S(2)}) copy-start(s32[32]{0:T(128)} %acount.3) | copy-start | bytes 388
  4.0 26.1 %collective-permute-start = (bf16[2,16,128,128]{3,2,1,0:T(8,128)(2,1)S(1)}, bf16[2,16,128,128]{3,2,1,0:T(8,128)(2,1)S(1)}, u32[]{:S(2)}, u32[]{:S(2)}) collective-permute-start(bf16[2,16,128,128]{3,2,1,0:T(8,128)(2,1)S(1)} %get-tuple-element.18.a0), channel_id=1, source_target_pairs={{0,1},{1,0},{2,3},{3,2},{4,5},{5,4},{6,7},{7,6},{8,9},{9,8},{10,11... | collective-permute-start | bytes 3145736 | tf_op jit(solution)/shard_map/ppermute | solution.py:436
  5.6 24.5 %collective-permute-start.1 = (bf16[2,16,128,128]{3,2,1,0:T(8,128)(2,1)S(1)}, bf16[2,16,128,128]{3,2,1,0:T(8,128)(2,1)S(1)}, u32[]{:S(2)}, u32[]{:S(2)}) collective-permute-start(bf16[2,16,128,128]{3,2,1,0:T(8,128)(2,1)S(1)} %get-tuple-element.19.b0), channel_id=1, source_target_pairs={{0,127},{1,2},{2,1},{3,4},{4,3},{5,6},{6,5},{7,8},{8,7},{9,10},{10... | collective-permute-start | bytes 3145736 | tf_op jit(solution)/shard_map/ppermute | solution.py:436
  17.9 21.2 %collective-permute-start.4 = (bf16[1,16,128,128]{3,2,1,0:T(8,128)(2,1)S(1)}, bf16[1,16,128,128]{3,2,1,0:T(8,128)(2,1)S(1)}, u32[]{:S(2)}, u32[]{:S(2)}) collective-permute-start(bf16[1,16,128,128]{3,2,1,0:T(8,128)(2,1)S(1)} %get-tuple-element.21.b1), channel_id=1, source_target_pairs={{0,127},{1,2},{2,1},{3,4},{4,3},{5,6},{6,5},{7,8},{8,7},{9,10},{10... | collective-permute-start | bytes 1572872 | tf_op jit(solution)/shard_map/ppermute | solution.py:438
  20.2 23.7 %collective-permute-start.3 = (bf16[1,16,128,128]{3,2,1,0:T(8,128)(2,1)S(1)}, bf16[1,16,128,128]{3,2,1,0:T(8,128)(2,1)S(1)}, u32[]{:S(2)}, u32[]{:S(2)}) collective-permute-start(bf16[1,16,128,128]{3,2,1,0:T(8,128)(2,1)S(1)} %get-tuple-element.20.a1), channel_id=1, source_target_pairs={{0,1},{1,0},{2,3},{3,2},{4,5},{5,4},{6,7},{7,6},{8,9},{9,8},{10,11... | collective-permute-start | bytes 1572872 | tf_op jit(solution)/shard_map/ppermute | solution.py:438
  31.2 14.3 %collective-permute-start.2 = (bf16[4,128,128]{2,1,0:T(8,128)(2,1)S(1)}, bf16[4,128,128]{2,1,0:T(8,128)(2,1)S(1)}, u32[]{:S(2)}, u32[]{:S(2)}) collective-permute-start(bf16[4,128,128]{2,1,0:T(8,128)(2,1)S(1)} %get-tuple-element.27), channel_id=1, source_target_pairs={{124,120},{120,116},{116,112},{112,108},{108,104},{104,100},{100,9... | collective-permute-start | bytes 393224 | tf_op jit(solution)/shard_map/ppermute | solution.py:444
  39.4 6.1 %collective-permute-start.5 = (bf16[1,128,128]{2,1,0:T(8,128)(2,1)S(1)}, bf16[1,128,128]{2,1,0:T(8,128)(2,1)S(1)}, u32[]{:S(2)}, u32[]{:S(2)}) collective-permute-start(bf16[1,128,128]{2,1,0:T(8,128)(2,1)S(1)} %shard_map.59.refs_4_), channel_id=1, source_target_pairs={{124,120},{120,116},{116,112},{112,108},{108,104},{104,100},{100,9... | collective-permute-start | bytes 98312 | tf_op jit(solution)/shard_map/ppermute | solution.py:444
  45.7 5.6 %collective-permute-start.7 = (bf16[2,11,32,128]{3,2,1,0:T(8,128)(2,1)S(1)}, bf16[2,11,32,128]{3,2,1,0:T(8,128)(2,1)S(1)}, u32[]{:S(2)}, u32[]{:S(2)}) collective-permute-start(bf16[2,11,32,128]{3,2,1,0:T(8,128)(2,1)S(1)} %get-tuple-element.29), channel_id=1, source_target_pairs={{0,1},{1,0},{2,3},{3,2},{4,5},{5,4},{6,7},{7,6},{8,9},{9,8},{10,11... | collective-permute-start | bytes 540680 | tf_op jit(solution)/shard_map/ppermute | solution.py:451
  46.5 10.9 %collective-permute-start.8 = (bf16[2,11,32,128]{3,2,1,0:T(8,128)(2,1)S(1)}, bf16[2,11,32,128]{3,2,1,0:T(8,128)(2,1)S(1)}, u32[]{:S(2)}, u32[]{:S(2)}) collective-permute-start(bf16[2,11,32,128]{3,2,1,0:T(8,128)(2,1)S(1)} %get-tuple-element.30), channel_id=1, source_target_pairs={{0,3},{1,2},{2,1},{3,0},{4,7},{5,6},{6,5},{7,4},{8,11},{9,10},{10,... | collective-permute-start | bytes 540680 | tf_op jit(solution)/shard_map/ppermute | solution.py:451
  49.8 9.3 %collective-permute-start.6 = (bf16[2,11,32,128]{3,2,1,0:T(8,128)(2,1)S(1)}, bf16[2,11,32,128]{3,2,1,0:T(8,128)(2,1)S(1)}, u32[]{:S(2)}, u32[]{:S(2)}) collective-permute-start(bf16[2,11,32,128]{3,2,1,0:T(8,128)(2,1)S(1)} %shard_map.61.refs_4_), channel_id=1, source_target_pairs={{0,2},{1,3},{2,0},{3,1},{4,6},{5,7},{6,4},{7,5},{8,10},{9,11},{10,... | collective-permute-start | bytes 540680 | tf_op jit(solution)/shard_map/ppermute | solution.py:451

commit v5 on v4

--- a/solution.py
+++ b/solution.py
@@ -387,10 +387,9 @@
 
 
 def gather_kernel(kinds, *refs):
-    parts = refs[: len(kinds)]
-    out_ref = refs[len(kinds)]
-    device, sub, parity = place()
-    out_ref[...] = jnp.zeros_like(out_ref)
+    parts, base, out_ref = refs[: len(kinds)], refs[len(kinds) : -1], refs[-1]
+    device, sub, parity = place()
+    out_ref[...] = base[0][...] if base else jnp.zeros_like(out_ref)
     for (d, groups), part in zip(kinds, parts, strict=True):
         first = 2 * (sub ^ d)
         at = 0
@@ -406,17 +405,17 @@
                 at += 1
 
 
-def gather_parts(kinds, parts):
+def gather_parts(kinds, parts, *base):
     def kernel(*refs):
         gather_kernel(kinds, *refs)
 
     return pl.pallas_call(
         kernel,
         out_shape=jax.ShapeDtypeStruct((8, 7, WIDE, TILE), F32),
-        in_specs=[VMEM] * len(parts),
+        in_specs=[VMEM] * (len(parts) + len(base)),
         out_specs=VMEM,
         compiler_params=pltpu.CompilerParams(vmem_limit_bytes=16 * MIB),
-    )(*parts)
+    )(*parts, *base)
 
 
 def shards(a_tiles, a_cols, a_count, p_tiles, p_cols):
@@ -451,7 +450,10 @@
                 part = lax.ppermute(part, "sub", [(i, i ^ d) for i in range(SUBS)])
             kinds.append((d, groups))
             parts.append(part)
-    return gather_parts(kinds, parts)
+    own = [n for n, (d, _) in enumerate(kinds) if d == 0]
+    far = [n for n, (d, _) in enumerate(kinds) if d > 0]
+    base = gather_parts([kinds[n] for n in own], [parts[n] for n in own])
+    return gather_parts([kinds[n] for n in far], [parts[n] for n in far], base)
 
 
 def solution(mesh):

time: 60.3 us -> 60.3 us (level)
    pallas_call x1 -> x2, Pallas kernels: 1.17 us -> 1.23 us  [gather_parts(): pl.pallas_call(kernel, out_shape=jax.ShapeDtypeStruct((8, 7, WIDE, TILE),...]
  transfers between devices with their start and end apart: 9 -> 9, of which waited for: 5 -> 4; matrix products, arithmetic and copies ran while one was open for 0% -> 0% of each run, Pallas kernels for 37% -> 37%
where the time goes in v5:
time: 60.3 us; the launch traced here: 60.2 us
  Pallas kernels  26.9 us (45%)
  starting transfers between devices  23.4 us (39%)
  waiting for transfers between devices  8.91 us (15%)
  local copies, waits for them, and re-layouts  0.85 us (1%)
    ppermute x2, starting transfers between devices, shards(): edges = [lax.ppermute(edge, both, hop) for edge in (edge0, edge1)]  12.4 us
    pallas_call x1, Pallas kernels, first_half(): pl.pallas_call(first_kernel, out_shape=[shape, shape] + LOCAL, in_specs=[...  10.6 us
    pallas_call x1, Pallas kernels, second_half(): pl.pallas_call(second_kernel, out_shape=LOCAL, in_specs=[SMEM, SMEM, HBM]...  9.39 us
    ppermute x3, waiting for transfers between devices, shards(): part = lax.ppermute(part, 'sub', [(i, i ^ d) for i in range(SUBS)])  7.81 us
    ppermute x3, starting transfers between devices, shards(): part = lax.ppermute(part, 'sub', [(i, i ^ d) for i in range(SUBS)])  5.47 us
    ppermute x2, starting transfers between devices, shards(): halo = [(lax.ppermute(a0, both, pairs_a), lax.ppermute(b0, both, pairs_b))]  3.26 us
    pallas_call x1, Pallas kernels, collapse(): pl.pallas_call(collapse_kernel, out_shape=[shape, shape], in_specs=[SMEM,...  3.11 us
    ppermute x1, starting transfers between devices, shards(): lax.ppermute(b1, both, pairs_b)  2.33 us
  transfers between devices with their start and end apart: 9, of which 4 were waited for; matrix products, arithmetic and copies ran while one was open for 0% of the time, Pallas kernels for 37%

profile of v5, /device:TPU:38, one launch (start us, length us, event | category | flops | bytes accessed | tf_op | source)
XLA Modules:
  0.0 60.2 jit_solution(2166330279638298912)
XLA Ops:
  0.0 0.8 %copy-done.1 = s32[32,4]{0,1:T(4,128)S(1)} copy-done((s32[32,4]{0,1:T(4,128)S(1)}, s32[32,4]{0,1:T(4,128)}, u32[]{:S(2)}) %copy-start.1) | copy-done | bytes 536
  0.8 3.1 %shard_map.55 = (bf16[2,16,128,128]{3,2,1,0:T(8,128)(2,1)S(1)}, bf16[2,16,128,128]{3,2,1,0:T(8,128)(2,1)S(1)}) custom-call(s32[4,32]{1,0:T(4,128)S(1)} %bitcast.2, bf16[32,4,128,128]{3,2,1,0:T(8,128)(2,1)} %p_hbm.3), custom_call_target="tpu_custom_call" | custom-call | flops 8388608 | bytes 6291456 | tf_op jit(solution)/shard_map/pallas_call | solution.py:89
  4.0 1.7 %collective-permute-start = (bf16[2,16,128,128]{3,2,1,0:T(8,128)(2,1)S(1)}, bf16[2,16,128,128]{3,2,1,0:T(8,128)(2,1)S(1)}, u32[]{:S(2)}, u32[]{:S(2)}) collective-permute-start(bf16[2,16,128,128]{3,2,1,0:T(8,128)(2,1)S(1)} %get-tuple-element.18.a0), channel_id=1, source_target_pairs={{0,1},{1,0},{2,3},{3,2},{4,5},{5,4},{6,7},{7,6},{8,9},{9,8},{10,11... | collective-permute-start | bytes 3145736 | tf_op jit(solution)/shard_map/ppermute | solution.py:435
  5.6 1.6 %collective-permute-start.1 = (bf16[2,16,128,128]{3,2,1,0:T(8,128)(2,1)S(1)}, bf16[2,16,128,128]{3,2,1,0:T(8,128)(2,1)S(1)}, u32[]{:S(2)}, u32[]{:S(2)}) collective-permute-start(bf16[2,16,128,128]{3,2,1,0:T(8,128)(2,1)S(1)} %get-tuple-element.19.b0), channel_id=1, source_target_pairs={{0,127},{1,2},{2,1},{3,4},{4,3},{5,6},{6,5},{7,8},{8,7},{9,10},{10... | collective-permute-start | bytes 3145736 | tf_op jit(solution)/shard_map/ppermute | solution.py:435
  7.2 10.6 %shard_map.56 = (bf16[1,16,128,128]{3,2,1,0:T(8,128)(2,1)S(1)}, bf16[1,16,128,128]{3,2,1,0:T(8,128)(2,1)S(1)}, f32[2,5,384,128]{3,2,1,0:T(8,128)S(1)}, bf16[2,384,2048]{2,1,0:T(8,128)(2,1)S(1)}) custom-call(s32[8,32]{1,0:T(8,128)S(1)} %bitcast.4, s32[32]{0:T(128)S(1)} %copy-done.4, s32[4,32]{1,0:T(4,128)S(1)} %bitcast.3, bf16[32,8,128,128]{3,2,1,0:T(8,128)(2,1)} %a_hbm.3, ...), custom_call_target="tpu_custom_call" | custom-call | flops 8589934592 | bytes 8388608 | tf_op jit(solution)/shard_map/pallas_call | solution.py:200
  17.9 2.3 %collective-permute-start.4 = (bf16[1,16,128,128]{3,2,1,0:T(8,128)(2,1)S(1)}, bf16[1,16,128,128]{3,2,1,0:T(8,128)(2,1)S(1)}, u32[]{:S(2)}, u32[]{:S(2)}) collective-permute-start(bf16[1,16,128,128]{3,2,1,0:T(8,128)(2,1)S(1)} %get-tuple-element.21.b1), channel_id=1, source_target_pairs={{0,127},{1,2},{2,1},{3,4},{4,3},{5,6},{6,5},{7,8},{8,7},{9,10},{10... | collective-permute-start | bytes 1572872 | tf_op jit(solution)/shard_map/ppermute | solution.py:437
  20.2 9.4 %shard_map.57 = (f32[2,5,384,128]{3,2,1,0:T(8,128)S(1)}, bf16[2,384,2048]{2,1,0:T(8,128)(2,1)S(1)}) custom-call(s32[8,32]{1,0:T(8,128)S(1)} %bitcast.5, s32[32]{0:T(128)S(1)} %copy-done.4, bf16[32,8,128,128]{3,2,1,0:T(8,128)(2,1)} %a_hbm.3, bf16[2,16,128,128]{3,2,1,0:T(8,128)(2,1)S(1)} %get-tuple-element.18.a0, ...), custom_call_target="tpu_custom_call", output_to_operand_aliasing={{0}: (7, {}), {1}: (8, {})} | custom-call | flops 8589934592 | bytes 8388608 | tf_op jit(solution)/shard_map/pallas_call | solution.py:219
  29.6 0.5 collective-permute-done.refs_0_
  30.1 0.0 collective-permute-done.1.refs_1_
  30.1 1.1 %shard_map.58 = (f32[2,8,128,128]{3,2,1,0:T(8,128)S(1)}, bf16[4,128,128]{2,1,0:T(8,128)(2,1)S(1)}) custom-call(bf16[2,16,128,128]{3,2,1,0:T(8,128)(2,1)S(1)} %collective-permute-done.refs_0_, bf16[2,16,128,128]{3,2,1,0:T(8,128)(2,1)S(1)} %collective-permute-done.1.refs_1_, bf16[2,384,2048]{2,1,0:T(8,128)(2,1)S(1)} %get-tuple-element.24.refs_2_.rh_ref, ...), custom_call_target="tpu_custom_call" | custom-call | flops 419430400 | bytes 6291456 | tf_op jit(solution)/shard_map/pallas_call | solution.py:333
  31.2 7.9 %collective-permute-start.2 = (bf16[4,128,128]{2,1,0:T(8,128)(2,1)S(1)}, bf16[4,128,128]{2,1,0:T(8,128)(2,1)S(1)}, u32[]{:S(2)}, u32[]{:S(2)}) collective-permute-start(bf16[4,128,128]{2,1,0:T(8,128)(2,1)S(1)} %get-tuple-element.27), channel_id=1, source_target_pairs={{124,120},{120,116},{116,112},{112,108},{108,104},{104,100},{100,9... | collective-permute-start | bytes 393224 | tf_op jit(solution)/shard_map/ppermute | solution.py:443
  39.1 0.0 collective-permute-done.4.hb_ref.refs_1_
  39.1 0.3 shard_map.59.refs_4_
  39.4 4.5 %collective-permute-start.5 = (bf16[1,128,128]{2,1,0:T(8,128)(2,1)S(1)}, bf16[1,128,128]{2,1,0:T(8,128)(2,1)S(1)}, u32[]{:S(2)}, u32[]{:S(2)}) collective-permute-start(bf16[1,128,128]{2,1,0:T(8,128)(2,1)S(1)} %shard_map.59.refs_4_), channel_id=1, source_target_pairs={{124,120},{120,116},{116,112},{112,108},{108,104},{104,100},{100,9... | collective-permute-start | bytes 98312 | tf_op jit(solution)/shard_map/ppermute | solution.py:443
  43.9 1.0 %shard_map.60.refs_2_ = f32[2,3,128,128]{3,2,1,0:T(8,128)S(1)} custom-call(bf16[1,16,128,128]{3,2,1,0:T(8,128)(2,1)S(1)} %collective-permute-done.3.refs_0_, bf16[1,16,128,128]{3,2,1,0:T(8,128)(2,1)S(1)} %collective-permute-done.4.hb_ref.refs_1_, bf16[2,384,2048]{2,1,0:T(8,128)(2,1)S(1)} %get-tuple-element.24.refs_2_.rh_ref, ...), custom_call_target="tpu_custom_call" | custom-call | flops 419430400 | bytes 6291456 | tf_op jit(solution)/shard_map/pallas_call | solution.py:333
  44.9 0.6 collective-permute-done.5.refs_3_
  45.5 0.1 shard_map.62
  45.7 0.9 %collective-permute-start.7 = (bf16[2,11,32,128]{3,2,1,0:T(8,128)(2,1)S(1)}, bf16[2,11,32,128]{3,2,1,0:T(8,128)(2,1)S(1)}, u32[]{:S(2)}, u32[]{:S(2)}) collective-permute-start(bf16[2,11,32,128]{3,2,1,0:T(8,128)(2,1)S(1)} %get-tuple-element.28), channel_id=1, source_target_pairs={{0,1},{1,0},{2,3},{3,2},{4,5},{5,4},{6,7},{7,6},{8,9},{9,8},{10,11... | collective-permute-start | bytes 540680 | tf_op jit(solution)/shard_map/ppermute | solution.py:450
  46.5 3.2 %collective-permute-start.8 = (bf16[2,11,32,128]{3,2,1,0:T(8,128)(2,1)S(1)}, bf16[2,11,32,128]{3,2,1,0:T(8,128)(2,1)S(1)}, u32[]{:S(2)}, u32[]{:S(2)}) collective-permute-start(bf16[2,11,32,128]{3,2,1,0:T(8,128)(2,1)S(1)} %get-tuple-element.29), channel_id=1, source_target_pairs={{0,3},{1,2},{2,1},{3,0},{4,7},{5,6},{6,5},{7,4},{8,11},{9,10},{10,... | collective-permute-start | bytes 540680 | tf_op jit(solution)/shard_map/ppermute | solution.py:450
  49.8 1.4 %collective-permute-start.6 = (bf16[2,11,32,128]{3,2,1,0:T(8,128)(2,1)S(1)}, bf16[2,11,32,128]{3,2,1,0:T(8,128)(2,1)S(1)}, u32[]{:S(2)}, u32[]{:S(2)}) collective-permute-start(bf16[2,11,32,128]{3,2,1,0:T(8,128)(2,1)S(1)} %shard_map.61.refs_4_), channel_id=1, source_target_pairs={{0,2},{1,3},{2,0},{3,1},{4,6},{5,7},{6,4},{7,5},{8,10},{9,11},{10,... | collective-permute-start | bytes 540680 | tf_op jit(solution)/shard_map/ppermute | solution.py:450
  51.1 0.1 shard_map.63.refs_3_
  51.3 6.2 %collective-permute-done.8.refs_2_ = bf16[2,11,32,128]{3,2,1,0:T(8,128)(2,1)S(1)} collective-permute-done((bf16[2,11,32,128]{3,2,1,0:T(8,128)(2,1)S(1)}, bf16[2,11,32,128]{3,2,1,0:T(8,128)(2,1)S(1)}, u32[]{:S(2)}, u32[]{:S(2)}) %collective-permute-start.8) | collective-permute-done | bytes 180256 | tf_op jit(solution)/shard_map/ppermute | solution.py:450
  57.4 1.7 %collective-permute-done.6.refs_0_ = bf16[2,11,32,128]{3,2,1,0:T(8,128)(2,1)S(1)} collective-permute-done((bf16[2,11,32,128]{3,2,1,0:T(8,128)(2,1)S(1)}, bf16[2,11,32,128]{3,2,1,0:T(8,128)(2,1)S(1)}, u32[]{:S(2)}, u32[]{:S(2)}) %collective-permute-start.6) | collective-permute-done | bytes 180256 | tf_op jit(solution)/shard_map/ppermute | solution.py:450
  59.1 1.1 %shard_map.64 = f32[8,7,32,128]{3,2,1,0:T(8,128)} custom-call(bf16[2,11,32,128]{3,2,1,0:T(8,128)(2,1)S(1)} %collective-permute-done.6.refs_0_, bf16[2,11,32,128]{3,2,1,0:T(8,128)(2,1)S(1)} %collective-permute-done.7.refs_1_, bf16[2,11,32,128]{3,2,1,0:T(8,128)(2,1)S(1)} %collective-permute-done.8.refs_2_, f32[8,7,32,128]{3,2,1,0:T(8,128)S(1)} %shard_map.63.refs_3_), custom_call_target="tpu_custom_call" | custom-call | tf_op jit(solution)/shard_map/pallas_call | solution.py:412
  (14 shorter events, 0.1 us)
Async XLA Ops:
  0.0 7.2 %copy-start = (bf16[32,4,128,128]{3,2,1,0:T(8,128)(2,1)S(1)}, bf16[32,4,128,128]{3,2,1,0:T(8,128)(2,1)}, u32[]{:S(2)}) copy-start(bf16[32,4,128,128]{3,2,1,0:T(8,128)(2,1)} %p_hbm.3) | copy-start | bytes 12582916
  0.0 0.8 %copy-start.1 = (s32[32,4]{0,1:T(4,128)S(1)}, s32[32,4]{0,1:T(4,128)}, u32[]{:S(2)}) copy-start(s32[32,4]{0,1:T(4,128)} %param.9) | copy-start | bytes 1540
  0.8 6.4 %copy-start.2 = (s32[32,4]{0,1:T(4,128)S(1)}, s32[32,4]{0,1:T(4,128)}, u32[]{:S(2)}) copy-start(s32[32,4]{0,1:T(4,128)} %param.9) | copy-start | bytes 1540
  0.8 6.4 %copy-start.3 = (s32[32,8]{0,1:T(8,128)S(1)}, s32[32,8]{0,1:T(8,128)}, u32[]{:S(2)}) copy-start(s32[32,8]{0,1:T(8,128)} %param.6) | copy-start | bytes 3076
  0.8 6.4 %copy-start.4 = (s32[32]{0:T(128)S(1)}, s32[32]{0:T(128)}, u32[]{:S(2)}) copy-start(s32[32]{0:T(128)} %acount.3) | copy-start | bytes 388
  4.0 26.1 %collective-permute-start = (bf16[2,16,128,128]{3,2,1,0:T(8,128)(2,1)S(1)}, bf16[2,16,128,128]{3,2,1,0:T(8,128)(2,1)S(1)}, u32[]{:S(2)}, u32[]{:S(2)}) collective-permute-start(bf16[2,16,128,128]{3,2,1,0:T(8,128)(2,1)S(1)} %get-tuple-element.18.a0), channel_id=1, source_target_pairs={{0,1},{1,0},{2,3},{3,2},{4,5},{5,4},{6,7},{7,6},{8,9},{9,8},{10,11... | collective-permute-start | bytes 3145736 | tf_op jit(solution)/shard_map/ppermute | solution.py:435
  5.6 24.5 %collective-permute-start.1 = (bf16[2,16,128,128]{3,2,1,0:T(8,128)(2,1)S(1)}, bf16[2,16,128,128]{3,2,1,0:T(8,128)(2,1)S(1)}, u32[]{:S(2)}, u32[]{:S(2)}) collective-permute-start(bf16[2,16,128,128]{3,2,1,0:T(8,128)(2,1)S(1)} %get-tuple-element.19.b0), channel_id=1, source_target_pairs={{0,127},{1,2},{2,1},{3,4},{4,3},{5,6},{6,5},{7,8},{8,7},{9,10},{10... | collective-permute-start | bytes 3145736 | tf_op jit(solution)/shard_map/ppermute | solution.py:435
  17.9 21.2 %collective-permute-start.4 = (bf16[1,16,128,128]{3,2,1,0:T(8,128)(2,1)S(1)}, bf16[1,16,128,128]{3,2,1,0:T(8,128)(2,1)S(1)}, u32[]{:S(2)}, u32[]{:S(2)}) collective-permute-start(bf16[1,16,128,128]{3,2,1,0:T(8,128)(2,1)S(1)} %get-tuple-element.21.b1), channel_id=1, source_target_pairs={{0,127},{1,2},{2,1},{3,4},{4,3},{5,6},{6,5},{7,8},{8,7},{9,10},{10... | collective-permute-start | bytes 1572872 | tf_op jit(solution)/shard_map/ppermute | solution.py:437
  20.2 23.7 %collective-permute-start.3 = (bf16[1,16,128,128]{3,2,1,0:T(8,128)(2,1)S(1)}, bf16[1,16,128,128]{3,2,1,0:T(8,128)(2,1)S(1)}, u32[]{:S(2)}, u32[]{:S(2)}) collective-permute-start(bf16[1,16,128,128]{3,2,1,0:T(8,128)(2,1)S(1)} %get-tuple-element.20.a1), channel_id=1, source_target_pairs={{0,1},{1,0},{2,3},{3,2},{4,5},{5,4},{6,7},{7,6},{8,9},{9,8},{10,11... | collective-permute-start | bytes 1572872 | tf_op jit(solution)/shard_map/ppermute | solution.py:437
  31.2 14.3 %collective-permute-start.2 = (bf16[4,128,128]{2,1,0:T(8,128)(2,1)S(1)}, bf16[4,128,128]{2,1,0:T(8,128)(2,1)S(1)}, u32[]{:S(2)}, u32[]{:S(2)}) collective-permute-start(bf16[4,128,128]{2,1,0:T(8,128)(2,1)S(1)} %get-tuple-element.27), channel_id=1, source_target_pairs={{124,120},{120,116},{116,112},{112,108},{108,104},{104,100},{100,9... | collective-permute-start | bytes 393224 | tf_op jit(solution)/shard_map/ppermute | solution.py:443
  39.4 6.1 %collective-permute-start.5 = (bf16[1,128,128]{2,1,0:T(8,128)(2,1)S(1)}, bf16[1,128,128]{2,1,0:T(8,128)(2,1)S(1)}, u32[]{:S(2)}, u32[]{:S(2)}) collective-permute-start(bf16[1,128,128]{2,1,0:T(8,128)(2,1)S(1)} %shard_map.59.refs_4_), channel_id=1, source_target_pairs={{124,120},{120,116},{116,112},{112,108},{108,104},{104,100},{100,9... | collective-permute-start | bytes 98312 | tf_op jit(solution)/shard_map/ppermute | solution.py:443
  45.7 5.6 %collective-permute-start.7 = (bf16[2,11,32,128]{3,2,1,0:T(8,128)(2,1)S(1)}, bf16[2,11,32,128]{3,2,1,0:T(8,128)(2,1)S(1)}, u32[]{:S(2)}, u32[]{:S(2)}) collective-permute-start(bf16[2,11,32,128]{3,2,1,0:T(8,128)(2,1)S(1)} %get-tuple-element.28), channel_id=1, source_target_pairs={{0,1},{1,0},{2,3},{3,2},{4,5},{5,4},{6,7},{7,6},{8,9},{9,8},{10,11... | collective-permute-start | bytes 540680 | tf_op jit(solution)/shard_map/ppermute | solution.py:450
  46.5 10.9 %collective-permute-start.8 = (bf16[2,11,32,128]{3,2,1,0:T(8,128)(2,1)S(1)}, bf16[2,11,32,128]{3,2,1,0:T(8,128)(2,1)S(1)}, u32[]{:S(2)}, u32[]{:S(2)}) collective-permute-start(bf16[2,11,32,128]{3,2,1,0:T(8,128)(2,1)S(1)} %get-tuple-element.29), channel_id=1, source_target_pairs={{0,3},{1,2},{2,1},{3,0},{4,7},{5,6},{6,5},{7,4},{8,11},{9,10},{10,... | collective-permute-start | bytes 540680 | tf_op jit(solution)/shard_map/ppermute | solution.py:450
  49.8 9.3 %collective-permute-start.6 = (bf16[2,11,32,128]{3,2,1,0:T(8,128)(2,1)S(1)}, bf16[2,11,32,128]{3,2,1,0:T(8,128)(2,1)S(1)}, u32[]{:S(2)}, u32[]{:S(2)}) collective-permute-start(bf16[2,11,32,128]{3,2,1,0:T(8,128)(2,1)S(1)} %shard_map.61.refs_4_), channel_id=1, source_target_pairs={{0,2},{1,3},{2,0},{3,1},{4,6},{5,7},{6,4},{7,5},{8,10},{9,11},{10,... | collective-permute-start | bytes 540680 | tf_op jit(solution)/shard_map/ppermute | solution.py:450
